TPU v7x, 32 devices: a whole 2x2x4 slice. The times are simulated.
32 devices in a mesh: dp: 8 (over z, y), fsdp: 4 (over x, core).
Axes of the slice: x: 2, y: 2, z: 4, core: 2. Of those that a mesh axis runs over, the one named last changes fastest.
Arguments:
- tokens: bfloat16 [32768, 768], P(('dp', 'fsdp')), may hold values from -6 to 6
- doc_ids: int32 [32768], P(('dp', 'fsdp')), may hold values from 0 to 4, as said below
- d_out: bfloat16 [32768, 768], P(('dp', 'fsdp')), may hold values from -6 to 6
- ln1_gain: bfloat16 [768], P(('dp', 'fsdp')), may hold values from 0.5 to 1.5
- ln1_shift: bfloat16 [768], P(('dp', 'fsdp')), may hold values from -1.5 to 1.5
- qkv_weight: bfloat16 [768, 2304], P(('dp', 'fsdp')), may hold values from -0.21875 to 0.21875
- qv_bias: bfloat16 [1536], P(('dp', 'fsdp')), may hold values from -1.5 to 1.5
- out_weight: bfloat16 [768, 768], P(('dp', 'fsdp')), may hold values from -0.625 to 0.625
- out_bias: bfloat16 [768], P(('dp', 'fsdp')), may hold values from -1.5 to 1.5
- ln2_gain: bfloat16 [768], P(('dp', 'fsdp')), may hold values from 0.5 to 1.5
- ln2_shift: bfloat16 [768], P(('dp', 'fsdp')), may hold values from -1.5 to 1.5
- fc_weight: bfloat16 [768, 3072], P(('dp', 'fsdp')), may hold values from -0.21875 to 0.21875
- fc_bias: bfloat16 [3072], P(('dp', 'fsdp')), may hold values from -1.5 to 1.5
- proj_weight: bfloat16 [3072, 768], P(('dp', 'fsdp')), may hold values from -0.109375 to 0.109375
- proj_bias: bfloat16 [768], P(('dp', 'fsdp')), may hold values from -1.5 to 1.5
Outputs:
- block_out: bfloat16 [32768, 768], P(('dp', 'fsdp'))
- input_grad: float32 [32768, 768], P(('dp', 'fsdp'))
- ln1_gain_grad: float32 [768], P(('dp', 'fsdp'))
- ln1_shift_grad: float32 [768], P(('dp', 'fsdp'))
- qkv_weight_grad: float32 [768, 2304], P(('dp', 'fsdp'))
- qv_bias_grad: float32 [1536], P(('dp', 'fsdp'))
- out_weight_grad: float32 [768, 768], P(('dp', 'fsdp'))
- out_bias_grad: float32 [768], P(('dp', 'fsdp'))
- ln2_gain_grad: float32 [768], P(('dp', 'fsdp'))
- ln2_shift_grad: float32 [768], P(('dp', 'fsdp'))
- fc_weight_grad: float32 [768, 3072], P(('dp', 'fsdp'))
- fc_bias_grad: float32 [3072], P(('dp', 'fsdp'))
- proj_weight_grad: float32 [3072, 768], P(('dp', 'fsdp'))
- proj_bias_grad: float32 [768], P(('dp', 'fsdp'))
Inputs may be any that keep to these rules, and one draw needn't show every extreme that they name: `doc_ids`: within each packed row of 1024 tokens (rows start at multiples of 1024) the ids start at 1, rise by one at each new document, never fall until the row's padding, and the row ends with one or more padding tokens of id 0; no document crosses a row's end; a row holds at most 4 documents, and some row holds exactly 4.
All inputs are finite; a program needn't handle non-finite values.
Results may differ from a plain program's by a relative error of at most 0.0088.
Values may be sent and summed in bfloat16 or wider, within the bound.
No kernel may reach another device: no remote copies, remote signals or barrier semaphores. Data moves between devices by JAX's collectives and lax.ppermute only.
A program may use at most 192 MiB of HBM per device.

v0:
```python
import functools
import math

import jax
import jax.numpy as jnp
from jax import lax
from jax.experimental import pallas as pl
from jax.experimental.pallas import tpu as pltpu
from jax.sharding import PartitionSpec as P

HD = 64
LEN = 1024
PAIR = 2 * HD
EPS = 1e-05
NEG = -1e30
AXES = ("dp", "fsdp")

F32 = jnp.float32
BF16 = jnp.bfloat16
NN = (((1,), (0,)), ((), ()))
NT = (((1,), (1,)), ((), ()))
TN = (((0,), (0,)), ((), ()))
ANY = pl.BlockSpec(memory_space=pl.ANY)
HBM = pl.BlockSpec(memory_space=pltpu.HBM)
SMEM = pl.BlockSpec(memory_space=pltpu.SMEM)

CORE, X, Y, Z0, Z1 = 1, 2, 4, 8, 16
CX, CY, CZ0, CZ1 = 1, 2, 4, 8
GROUPS = tuple(tuple(near | far for far in (0, CZ0, CZ1, CZ0 | CZ1)) for near in (0, CX, CY, CX | CY))


def dot(a, b, dims):
    return lax.dot_general(a, b, dims, preferred_element_type=F32)


def params(size):
    return pltpu.CompilerParams(vmem_limit_bytes=size << 20)


def cost(flops, size):
    return pl.CostEstimate(flops=int(flops), bytes_accessed=int(size), transcendentals=0)


def whole(shape):
    return pl.BlockSpec(shape, lambda *g: (0,) * len(shape))


def rows(block, width):
    return pl.BlockSpec((block, width), lambda i: (i, 0))


def swap(array, bit):
    count = lax.axis_size("dp") * lax.axis_size("fsdp")
    return lax.ppermute(array, AXES, [(i, i ^ bit) for i in range(count)])


def halves(array, core):
    width = array.shape[1] // 2
    low, high = array[:, :width], array[:, width:]
    first = core == 0
    return jnp.where(first, low, high), jnp.where(first, high, low)


def pair_block(array, core, extra=None):
    keep, send = halves(array, core)
    if extra is not None:
        keep, send = jnp.concatenate([keep, extra], 1), jnp.concatenate([send, extra], 1)
    other = swap(send, CORE)
    first = core == 0
    return jnp.concatenate([jnp.where(first, keep, other), jnp.where(first, other, keep)], 0)


def by_z(parts):
    return [swap(part, bits) for part, bits in zip(parts, (Z0, Z1, Z0 | Z1))]


def by_xy(parts):
    return [swap(part, bits) for part, bits in zip(parts, (X, Y, X | Y))]


def gather_core(own):
    return [*own, *(swap(piece, CORE) for piece in own)]


def add(*terms):
    return functools.reduce(lambda a, b: a + b, [t.astype(F32) for t in terms])


def scatter_core(terms):
    mine, other = terms
    got = swap(other, CORE)
    return [add(mine[g], got[g]).astype(BF16) for g in range(4)]


def sum_xy(sums, got):
    return [add(*(part[spot] for part in [sums[0], *got])).astype(BF16) for spot in range(4)]


def tie(arrays, *others):
    if not others:
        return list(arrays)
    return list(lax.optimization_barrier((*arrays, *others))[: len(arrays)])


def meet(*lists):
    found = iter(lax.optimization_barrier(tuple(array for arrays in lists for array in arrays)))
    return [[next(found) for _ in arrays] for arrays in lists]


def kernel_call(kernel, inputs, after, **how):
    return pl.pallas_call(kernel, **how)(*tie(inputs[:1], *after), *inputs[1:])


def own_rows(block, core):
    count = block.shape[0] // 2
    low, high = block[:count], block[count:]
    first = core == 0
    keep = jnp.where(first, low, high)
    got = swap(jnp.where(first, high, low), CORE)
    return jnp.where(first, keep, got), jnp.where(first, got, keep)


def gather_all(array):
    return lax.all_gather(array, AXES, axis=0, tiled=True)


def scatter_all(array):
    return lax.psum_scatter(array, AXES, scatter_dimension=0, tiled=True)


def scatter_small(table, index, bits):
    for bit in bits:
        count = table.shape[0] // 2
        low = (index & bit) == 0
        keep = jnp.where(low, table[:count], table[count:])
        send = jnp.where(low, table[count:], table[:count])
        table = keep + swap(send, bit)
    return table


def fetch(place, pieces, which, lane, width, into, sem):
    if len(pieces) < 8:
        pltpu.make_async_copy(pieces[which], into, sem).start()
        return lambda: pltpu.make_async_copy(into, into, sem).wait()
    chip, core = place[0], place[1]
    step = into.shape[0] // 16
    for side in range(2):
        half = core if side == 0 else 1 - core
        column = pl.ds(pl.multiple_of(half * width, 128), width)
        for group in range(4):
            for spot, relative in enumerate(GROUPS[group]):
                owner = lax.bitwise_xor(chip, relative)
                pltpu.make_async_copy(
                    pieces[4 * side + group].at[spot, :, pl.ds(lane, width)],
                    into.at[pl.ds(pl.multiple_of(owner * step, step), step), column],
                    sem,
                ).start()
    return lambda: pltpu.make_async_copy(into, into, sem).wait()


def normal(v):
    center = v - jnp.mean(v, -1, keepdims=True)
    spread = jnp.mean(center * center, -1, keepdims=True)
    factor = lax.rsqrt(spread + EPS)
    return center * factor, factor


def one_hot(shape, base, span, first):
    lane = lax.broadcasted_iota(jnp.int32, shape, 0)
    element = lax.broadcasted_iota(jnp.int32, (1, shape[1]), 1) + first
    return lane == base + lax.rem(element, span)


def owner(shape, span, first):
    element = lax.broadcasted_iota(jnp.int32, (1, shape[1]), 1) + first
    return lax.broadcasted_iota(jnp.int32, shape, 0) == element // span


def unpack_rows(table, out, lanes):
    devices, full = table.shape
    width = out.shape[1]
    unit = lanes // 12
    wide = table.astype(F32)
    spans = (1, 1, 2, 1, 1, 1, 4, 1)
    for span in (1, 2, 4):
        starts = [sum(spans[:i]) for i, one in enumerate(spans) if one == span]
        parts = [
            (wide if start == 0 else pltpu.roll(wide, full - start * unit, 1))[:, :128].astype(BF16) for start in starts
        ]
        pick = one_hot((128, width), 0, span * unit, 0).astype(BF16)
        values = dot(jnp.concatenate(parts, 0), pick, NN)
        for index, start in enumerate(starts):
            value = values[index * devices : (index + 1) * devices]
            for row in range(span):
                mine = owner((devices, width), span * unit, row * width)
                out[start + row : start + row + 1, :] = jnp.sum(jnp.where(mine, value, 0.0), 0, keepdims=True)


def unpack_blocks(place, pieces, out, kept, sem):
    lane = pieces[0].shape[2] - 128
    chip = place[0]
    step = pieces[0].shape[1]
    for group in range(4):
        for spot, relative in enumerate(GROUPS[group]):
            there = pl.ds(pl.multiple_of(lax.bitwise_xor(chip, relative) * step, step), step)
            pltpu.make_async_copy(pieces[group].at[spot, :, pl.ds(lane, 128)], kept.at[there, :], sem).start()
    finish(kept, sem)
    width = out.shape[1]
    devices = width // (step // 2)
    lanes = 12 * step // 2
    parts = []
    for part in range(-(-lanes // 128)):
        shape = (devices, width)
        device = lax.broadcasted_iota(jnp.int32, shape, 0)
        pick = lax.broadcasted_iota(jnp.int32, shape, 1) == device * (step // 2) + part
        parts.append(dot(pick.astype(BF16), kept[...], NN).astype(BF16))
    unpack_rows(jnp.concatenate(parts, 1), out, lanes)


def allowed(q_doc, k_doc, first, shape, q_dim):
    q_pos = lax.broadcasted_iota(jnp.int32, shape, q_dim) + first
    k_pos = lax.broadcasted_iota(jnp.int32, shape, 1 - q_dim)
    allow = ((k_pos <= q_pos) & (q_doc == k_doc) & (k_doc > 0)) | (k_pos == q_pos)
    return jnp.where(allow, 0.0, NEG)


def project_attend_kernel(steps, block, place, x, q_docs, k_docs, *rest):
    pieces, rest = rest[:-12], rest[-12:]
    mixed, hidden, out, lse, vectors, kept, bias, weight, small, sem, kept_sem, small_sem = rest
    width = x.shape[1]
    size = x.shape[0]
    step = pl.program_id(0)

    @pl.when(step == 0)
    def _():
        wait = fetch(place, pieces, 0, 0, 3 * width // 2, weight, sem)
        if len(pieces) == 8:
            unpack_blocks(place, pieces[:4], vectors, small, small_sem)
        else:
            unpack_rows(pieces[1][...], vectors, 12 * vectors.shape[1] // pieces[1].shape[0])
        for i in range(LEN // block):
            sl, reach = slice(i * block, (i + 1) * block), (i + 1) * block
            bias[sl, :reach] = allowed(q_docs[sl, :], k_docs[:, :reach], i * block, (block, reach), 0)
        wait()

    @pl.when(step < steps)
    def _():
        unit, _ = normal(x[...].astype(F32))
        h = (unit * vectors[0:1, :] + vectors[1:2, :]).astype(BF16)
        hidden[...] = h
        scale = 1.0 / math.sqrt(HD)
        here = pl.ds(pl.multiple_of(step * size, size), size)
        for part in range(3):
            sl = slice(part * width, (part + 1) * width)
            value = dot(h, weight[:, sl], NN)
            if part == 0:
                value = (value + vectors[2:3, :]).astype(BF16).astype(F32) * scale
            if part == 2:
                value = value + vectors[3:4, :]
            kept[here, sl] = value.astype(BF16)
        pltpu.make_async_copy(kept.at[here, :], mixed.at[here, :], kept_sem).start()

    @pl.when(step >= steps)
    def _():
        lane = (step - steps) * PAIR
        q_at, k_at, v_at = (pl.ds(pl.multiple_of(lane + part * width, PAIR), PAIR) for part in range(3))
        low = lax.broadcasted_iota(jnp.int32, (block, PAIR), 1) < HD
        for i in range(LEN // block):
            sl, reach = slice(i * block, (i + 1) * block), (i + 1) * block
            q = kept[sl, q_at]
            outs, logs = [], []
            for head in range(2):
                q_one = jnp.where(low if head == 0 else ~low, q, jnp.zeros_like(q))
                score = dot(q_one, kept[:reach, k_at], NT) + bias[sl, :reach]
                top = jnp.max(score, -1, keepdims=True)
                expo = jnp.exp(score - top)
                total = jnp.sum(expo, -1, keepdims=True)
                outs.append(dot(expo.astype(BF16), kept[:reach, v_at], NN) / total)
                logs.append(top + jnp.log(total))
            out[sl, :] = jnp.where(low, outs[0], outs[1]).astype(BF16)
            turned = jnp.where(low, logs[0], logs[1]).T
            lse[0, 0:1, sl] = turned[0:1, :]
            lse[0, 1:2, sl] = turned[HD : HD + 1, :]

    @pl.when(step == pl.num_programs(0) - 1)
    def _():
        finish(kept, kept_sem)


def project_attend(place, x, docs, pieces, after=()):
    count, width = x.shape
    size, block = 256, 512
    steps = count // size
    pairs = width // PAIR
    early = lambda i: (jnp.minimum(i, steps - 1), 0)
    late = lambda i: jnp.maximum(i - steps, 0)
    return kernel_call(
        functools.partial(project_attend_kernel, steps, block),
        [place, x, docs.reshape(LEN, 1), docs.reshape(1, LEN), *pieces],
        after,
        grid=(steps + pairs,),
        in_specs=[SMEM, pl.BlockSpec((size, width), early), whole((LEN, 1)), whole((1, LEN))]
        + ([HBM] * 8 if len(pieces) == 8 else [HBM, whole(pieces[1].shape)]),
        out_specs=[
            HBM,
            pl.BlockSpec((size, width), early),
            pl.BlockSpec((LEN, PAIR), lambda i: (0, late(i))),
            pl.BlockSpec((1, 2, LEN), lambda i: (late(i), 0, 0)),
            whole((12, width)),
        ],
        out_shape=[
            pltpu.HBM((count, 3 * width), BF16),
            pltpu.HBM((count, width), BF16),
            jax.ShapeDtypeStruct((count, width), BF16),
            jax.ShapeDtypeStruct((pairs, 2, LEN), F32),
            jax.ShapeDtypeStruct((12, width), F32),
        ],
        scratch_shapes=[
            pltpu.VMEM((count, 3 * width), BF16),
            pltpu.VMEM((LEN, LEN), F32),
            pltpu.VMEM((width, 3 * width), BF16),
            pltpu.VMEM((width, 128), BF16),
            pltpu.SemaphoreType.DMA,
            pltpu.SemaphoreType.DMA,
            pltpu.SemaphoreType.DMA,
        ],
        compiler_params=params(26),
        cost_estimate=cost(28e9, 20e6),
        name="project_attend",
    )


def norm_back(v, gain, grad):
    unit, factor = normal(v)
    g = grad * gain
    pulled = factor * (g - jnp.mean(g, -1, keepdims=True) - unit * jnp.mean(g * unit, -1, keepdims=True))
    return pulled, jnp.sum(grad * unit, 0, keepdims=True), jnp.sum(grad, 0, keepdims=True)


def send(place, tile, column, width, outs, lane, half, first, sem):
    here = pl.ds(column, width)
    if len(outs) == 1:
        per_half = outs[0].shape[1] // 2
        at = pl.ds(pl.multiple_of(half * per_half + lane, 128), width)
        top = pl.ds(pl.multiple_of(first * (outs[0].shape[0] // 16), 16), tile.shape[0])
        pltpu.make_async_copy(tile.at[:, here], outs[0].at[top, at], sem).start()
        return
    chip, core = place[0], place[1]
    step = outs[0].shape[2]
    at = pl.ds(pl.multiple_of(lane, 128), width)
    for index in range(tile.shape[0] // step):
        relative = lax.bitwise_xor(chip, first + index)
        group, spot = lax.bitwise_and(relative, 3), lax.shift_right_logical(relative, 2)
        source = tile.at[pl.ds(index * step, step), here]
        for own, target in ((True, outs[0]), (False, outs[1])):
            copy = pltpu.make_async_copy(source, target.at[group, spot, :, at], sem)
            pl.when((half == core) == own)(copy.start)


def finish(ref, sem):
    pltpu.make_async_copy(ref, ref, sem).wait()


def term_shapes(tall, wide, by_stage):
    if by_stage:
        return [jax.ShapeDtypeStruct((4, 4, tall // 16, wide // 2), BF16)] * 2
    return [jax.ShapeDtypeStruct((tall, wide), BF16)]


def widen_kernel(steps, terms, place, x, attended, out_bias, gain, shift, fc_bias, cot, *rest):
    count = terms + 15
    pieces, rest = rest[:-count], rest[-count:]
    resid, hidden, slope, active = rest[:4]
    outs, rest = rest[4 : 4 + terms], rest[4 + terms :]
    w_out, w_fc, kept, bent, grad, stage, weight_sems, kept_sem, bent_sem, grad_sem, sems = rest
    size, width = x.shape
    depth = w_fc.shape[1]
    step = pl.program_id(0)
    here = pl.ds(pl.multiple_of(lax.rem(step, steps) * size, size), size)

    @pl.when(step == 0)
    def _():
        wait_out = fetch(place, pieces, 0, 0, width // 2, w_out, weight_sems.at[0])
        wait_fc = fetch(place, pieces, 1, width // 2, depth // 2, w_fc, weight_sems.at[1])
        pltpu.make_async_copy(cot, grad, grad_sem).start()
        wait_out()
        wait_fc()

    @pl.when(step < steps)
    def _():
        r = x[...].astype(F32) + dot(attended[...], w_out[...], NN) + out_bias[...]
        resid[...] = r
        unit, _ = normal(r)
        h = (unit * gain[...] + shift[...]).astype(BF16)
        hidden[...] = h
        c = math.sqrt(2.0 / math.pi)
        for first in range(0, depth, width):
            sl = slice(first, first + width)
            u = dot(h, w_fc[:, sl], NN) + fc_bias[:, sl]
            bend = (c * 0.044715) * (u * u) + c
            half = 0.5 * jnp.tanh(u * bend) + 0.5
            value = u * half
            kept[here, sl] = value.astype(BF16)
            bent[here, sl] = (half + value * (1.0 - half) * (6.0 * bend - 4.0 * c)).astype(BF16)
        pltpu.make_async_copy(kept.at[here, :], active.at[here, :], kept_sem).start()
        pltpu.make_async_copy(bent.at[here, :], slope.at[here, :], bent_sem).start()

    @pl.when(step >= steps)
    def _():
        tile = step - steps
        slot = lax.rem(tile, 2)

        @pl.when(tile == 0)
        def _():
            finish(grad, grad_sem)

        @pl.when(tile >= 2)
        def _():
            finish(stage.at[slot], sems.at[slot])

        tall = stage.shape[1]
        part = kept[:, pl.ds(pl.multiple_of(tile * tall, tall), tall)]
        stage[slot] = dot(part, grad[...], TN).astype(BF16)
        chips = tall * 16 // depth
        for half in range(2):
            send(place, stage.at[slot], half * (width // 2), width // 2, outs, 0, half, tile * chips, sems.at[slot])

        @pl.when(tile == depth // tall - 1)
        def _():
            finish(stage.at[slot], sems.at[slot])
            finish(stage.at[1 - slot], sems.at[1 - slot])
            finish(kept, kept_sem)
            finish(bent, bent_sem)


def widen(place, x, attended, out_bias, gain, shift, fc_bias, cot, pieces, after=()):
    count, width = x.shape
    depth = fc_bias.shape[1]
    size, tall = 256, width
    steps = count // size
    early = lambda i: (jnp.minimum(i, steps - 1), 0)
    block = lambda wide: pl.BlockSpec((size, wide), early)
    terms = term_shapes(depth, width, len(pieces) == 8)
    return kernel_call(
        functools.partial(widen_kernel, steps, len(terms)),
        [place, x, attended, out_bias, gain, shift, fc_bias, cot, *pieces],
        after,
        grid=(steps + depth // tall,),
        in_specs=[SMEM, block(width), block(width)]
        + [whole((1, width))] * 3
        + [whole((1, depth)), ANY]
        + [HBM] * len(pieces),
        out_specs=[block(width), block(width), HBM, HBM] + [ANY] * len(terms),
        out_shape=[
            pltpu.HBM((count, width), F32),
            jax.ShapeDtypeStruct((count, width), BF16),
            pltpu.HBM((count, depth), BF16),
            pltpu.HBM((count, depth), BF16),
        ]
        + terms,
        scratch_shapes=[
            pltpu.VMEM((width, width), BF16),
            pltpu.VMEM((width, depth), BF16),
            pltpu.VMEM((count, depth), BF16),
            pltpu.VMEM((count, depth), BF16),
            pltpu.VMEM((count, width), BF16),
            pltpu.VMEM((2, tall, width), BF16),
            pltpu.SemaphoreType.DMA((2,)),
            pltpu.SemaphoreType.DMA,
            pltpu.SemaphoreType.DMA,
            pltpu.SemaphoreType.DMA,
            pltpu.SemaphoreType.DMA((2,)),
        ],
        compiler_params=params(32),
        cost_estimate=cost(2 * count * width * (width + 2 * depth), 30e6),
        name="widen",
    )


def narrow_kernel(steps, terms, sides, place, resid, active, slope, cot, proj_bias, gain, hidden, attended, *rest):
    count = terms + 19
    pieces, rest = rest[:-count], rest[-count:]
    wide_pieces, proj_pieces = pieces[:sides], pieces[sides:]
    result, grad_r, grad_o, fc_sum, proj_sum, gain_sum, shift_sum, bias_sum = rest[:8]
    outs, rest = rest[8 : 8 + terms], rest[8 + terms :]
    w_proj, w_fc, w_out, du, dt, h_kept, o_kept, stage, weight_sems, kept_sems, sems = rest
    size, width = resid.shape
    depth = active.shape[1]
    step = pl.program_id(0)
    here = pl.ds(pl.multiple_of(lax.rem(step, steps) * size, size), size)

    @pl.when(step == 0)
    def _():
        wait_proj = fetch(place, proj_pieces, 0, 0, width // 2, w_proj, weight_sems.at[0])
        wait_fc = fetch(place, wide_pieces, 1, width // 2, depth // 2, w_fc, weight_sems.at[1])
        wait_out = fetch(place, wide_pieces, 0, 0, width // 2, w_out, weight_sems.at[2])
        pltpu.make_async_copy(hidden, h_kept, kept_sems.at[0]).start()
        pltpu.make_async_copy(attended, o_kept, kept_sems.at[1]).start()
        for total in (fc_sum, proj_sum, gain_sum, shift_sum, bias_sum):
            total[...] = jnp.zeros_like(total)
        wait_proj()
        wait_fc()
        wait_out()

    @pl.when(step < steps)
    def _():
        g = cot[...]
        for first in range(0, depth, width):
            sl = slice(first, first + width)
            part = (dot(g, w_proj[sl, :], NT) * slope[:, sl].astype(F32)).astype(BF16)
            du[here, sl] = part
            fc_sum[:, sl] += jnp.sum(part.astype(F32), 0, keepdims=True)
        r = resid[...]
        result[...] = (r + dot(active[...], w_proj[...], NN) + proj_bias[...]).astype(BF16)
        wide = g.astype(F32)
        proj_sum[...] += jnp.sum(wide, 0, keepdims=True)
        grad_h = dot(du[here, :], w_fc[...], NT)
        pulled, gains, shifts = norm_back(r, gain[...], grad_h)
        total = wide + pulled
        grad_r[...] = total
        low = total.astype(BF16)
        dt[here, :] = low
        gain_sum[...] += gains
        shift_sum[...] += shifts
        bias_sum[...] += jnp.sum(low.astype(F32), 0, keepdims=True)
        grad_o[...] = dot(low, w_out[...], NT).astype(BF16)

    tiles = depth // width

    @pl.when(step >= steps)
    def _():
        tile = step - steps
        slot = lax.rem(tile, 2)

        @pl.when(tile == 0)
        def _():
            finish(h_kept, kept_sems.at[0])
            finish(o_kept, kept_sems.at[1])

        @pl.when(tile >= 2)
        def _():
            finish(stage.at[slot], sems.at[slot])

        @pl.when(tile < tiles)
        def _():
            part = du[:, pl.ds(pl.multiple_of(lax.rem(tile, tiles) * width, width), width)]
            stage[slot] = dot(h_kept[...], part, TN).astype(BF16)
            lane = lax.rem(tile, tiles // 2) * width
            send(place, stage.at[slot], 0, width, outs, lane, tile // (tiles // 2), 0, sems.at[slot])

        @pl.when(tile == tiles)
        def _():
            stage[slot] = dot(o_kept[...], dt[...], TN).astype(BF16)
            for half in range(2):
                send(place, stage.at[slot], half * (width // 2), width // 2, outs, depth // 2, half, 0, sems.at[slot])
            finish(stage.at[slot], sems.at[slot])
            finish(stage.at[1 - slot], sems.at[1 - slot])


def narrow(place, resid, active, slope, cot, proj_bias, gain, hidden, attended, wide_pieces, proj_pieces, after=()):
    count, width = resid.shape
    depth = active.shape[1]
    size = 256
    steps = count // size
    early = lambda i: (jnp.minimum(i, steps - 1), 0)
    block = lambda wide: pl.BlockSpec((size, wide), early)
    pieces = [*wide_pieces, *proj_pieces]
    terms = term_shapes(width, width + depth, len(proj_pieces) == 8)
    return kernel_call(
        functools.partial(narrow_kernel, steps, len(terms), len(wide_pieces)),
        [place, resid, active, slope, cot, proj_bias, gain, hidden, attended, *pieces],
        after,
        grid=(steps + depth // width + 1,),
        in_specs=[SMEM, block(width), block(depth), block(depth), block(width)]
        + [whole((1, width))] * 2
        + [ANY] * 2 + [HBM] * len(pieces),
        out_specs=[block(width)] * 3
        + [whole((1, depth))]
        + [whole((1, width))] * 4
        + [ANY] * len(terms),
        out_shape=[
            jax.ShapeDtypeStruct((count, width), BF16),
            jax.ShapeDtypeStruct((count, width), F32),
            jax.ShapeDtypeStruct((count, width), BF16),
            jax.ShapeDtypeStruct((1, depth), F32),
        ]
        + [jax.ShapeDtypeStruct((1, width), F32)] * 4
        + terms,
        scratch_shapes=[
            pltpu.VMEM((depth, width), BF16),
            pltpu.VMEM((width, depth), BF16),
            pltpu.VMEM((width, width), BF16),
            pltpu.VMEM((count, depth), BF16),
            pltpu.VMEM((count, width), BF16),
            pltpu.VMEM((count, width), BF16),
            pltpu.VMEM((count, width), BF16),
            pltpu.VMEM((2, width, width), BF16),
            pltpu.SemaphoreType.DMA((3,)),
            pltpu.SemaphoreType.DMA((2,)),
            pltpu.SemaphoreType.DMA((2,)),
        ],
        compiler_params=params(40),
        cost_estimate=cost(2 * count * width * (2 * width + 4 * depth), 40e6),
        name="narrow",
    )


def attend_back_kernel(block, number, terms, place, q_docs, k_docs, q_all, k_all, v_all, o_all, g_all, lse, hidden, *rest):
    dq, dk, dv = rest[:3]
    outs, rest = rest[3 : 3 + terms], rest[3 + terms :]
    bias, k_sum, v_sum, kept, h_kept, stage, sem, sems = rest
    count = LEN // block
    step = pl.program_id(0)

    @pl.when(step == 0)
    def _():
        pltpu.make_async_copy(hidden, h_kept, sem).start()
        for i in range(count):
            sl, reach = slice(i * block, (i + 1) * block), (i + 1) * block
            bias[:reach, sl] = allowed(q_docs[:, sl], k_docs[:reach, :], i * block, (reach, block), 1)

    @pl.when(step < number)
    def _():
        low = lax.broadcasted_iota(jnp.int32, (block, PAIR), 1) < HD
        low_all = lax.broadcasted_iota(jnp.int32, (LEN, PAIR), 1) < HD
        keys = k_all[...]
        key_one = [jnp.where(low_all, keys, jnp.zeros_like(keys)), jnp.where(low_all, jnp.zeros_like(keys), keys)]
        at = pl.ds(pl.multiple_of(lax.rem(step, number) * PAIR, PAIR), PAIR)
        for i in reversed(range(count)):
            sl, reach = slice(i * block, (i + 1) * block), (i + 1) * block
            q, grad = q_all[sl, :], g_all[sl, :]
            turned = (grad.astype(F32) * o_all[sl, :].astype(F32)).T
            parts = []
            for head in range(2):
                lane = low if head == 0 else ~low
                q_one = jnp.where(lane, q, jnp.zeros_like(q))
                g_one = jnp.where(lane, grad, jnp.zeros_like(grad))
                inner = jnp.sum(turned[head * HD : (head + 1) * HD, :], 0, keepdims=True)
                score = dot(k_all[:reach, :], q_one, NT) + bias[:reach, sl]
                prob = jnp.exp(score - lse[0, head : head + 1, sl])
                v_part = dot(prob.astype(BF16), g_one, NN)
                slope = dot(v_all[:reach, :], g_one, NT)
                dscore = (prob * (slope - inner)).astype(BF16)
                k_part = dot(dscore, q_one, NN)
                if i == count - 1 and head == 0:
                    k_sum[...] = k_part
                    v_sum[...] = v_part
                else:
                    k_sum[:reach, :] += k_part
                    v_sum[:reach, :] += v_part
                parts.append(dot(dscore, key_one[head][:reach], TN))
            part = ((parts[0] + parts[1]) * (1.0 / math.sqrt(HD))).astype(BF16)
            dq[sl, :] = part
            kept[0, sl, at] = part
        for index, (ref, total) in enumerate(((dk, k_sum), (dv, v_sum))):
            part = total[...].astype(BF16)
            ref[...] = part
            kept[1 + index, :, at] = part

    wide = stage.shape[3]

    @pl.when(step >= number)
    def _():
        tile = step - number
        slot = lax.rem(tile, 2)

        @pl.when(tile == 0)
        def _():
            finish(h_kept, sem)

        @pl.when(tile >= 2)
        def _():
            finish(stage.at[slot], sems.at[slot])

        for index in range(3):
            part = kept[index, :, pl.ds(pl.multiple_of(tile * wide, wide), wide)]
            stage[slot, index] = dot(h_kept[...], part, TN).astype(BF16)
        for index in range(3):
            for half in range(2):
                send(
                    place,
                    stage.at[slot, index],
                    half * (wide // 2),
                    wide // 2,
                    outs,
                    index * (number * PAIR // 2) + tile * (wide // 2),
                    half,
                    0,
                    sems.at[slot],
                )

        @pl.when(tile == number * PAIR // wide - 1)
        def _():
            finish(stage.at[slot], sems.at[slot])
            if number * PAIR // wide > 1:
                finish(stage.at[1 - slot], sems.at[1 - slot])


def attend_back(place, mixed, attended, grad_o, lse, docs, hidden, by_stage, after=()):
    width = attended.shape[1]
    number = width // PAIR
    block = 256
    wide = 2 * PAIR
    steps = width // wide
    pair = lambda i: jnp.minimum(i, number - 1)
    column = lambda base: pl.BlockSpec((LEN, PAIR), lambda i: (0, base + pair(i)))
    terms = term_shapes(width, 3 * number * PAIR, by_stage)
    return kernel_call(
        functools.partial(attend_back_kernel, block, number, len(terms)),
        [place, docs.reshape(1, LEN), docs.reshape(LEN, 1), mixed, mixed, mixed, attended, grad_o, lse, hidden],
        after,
        grid=(number + steps,),
        in_specs=[
            SMEM,
            whole((1, LEN)),
            whole((LEN, 1)),
            column(0),
            column(number),
            column(2 * number),
            column(0),
            column(0),
            pl.BlockSpec((1, 2, LEN), lambda i: (pair(i), 0, 0)),
            ANY,
        ],
        out_specs=[column(0)] * 3 + [ANY] * len(terms),
        out_shape=[jax.ShapeDtypeStruct((LEN, PAIR * number), BF16)] * 3 + terms,
        scratch_shapes=[
            pltpu.VMEM((LEN, LEN), F32),
            pltpu.VMEM((LEN, PAIR), F32),
            pltpu.VMEM((LEN, PAIR), F32),
            pltpu.VMEM((3, LEN, PAIR * number), BF16),
            pltpu.VMEM((LEN, width), BF16),
            pltpu.VMEM((2, 3, width, wide), BF16),
            pltpu.SemaphoreType.DMA,
            pltpu.SemaphoreType.DMA((2,)),
        ],
        compiler_params=params(56),
        cost_estimate=cost(42e9, 20e6),
        name="attend_back",
    )


def first_back_kernel(place, x, grad_r, gain, *rest):
    parts, pieces, rest = rest[:3], rest[3:-4], rest[-4:]
    grad_x, sums, weight, sem = rest
    width = x.shape[1]

    @pl.when(pl.program_id(0) == 0)
    def _():
        fetch(place, pieces, 0, 0, 3 * width // 2, weight, sem)()
        sums[...] = jnp.zeros_like(sums)

    grad_h = dot(parts[0][...], weight[:, :width], NT)
    for index in (1, 2):
        grad_h += dot(parts[index][...], weight[:, index * width : (index + 1) * width], NT)
    for at, part in ((2, parts[0]), (3, parts[2])):
        sums[at : at + 1, :] += jnp.sum(part[...].astype(F32), 0, keepdims=True)
    pulled, gains, shifts = norm_back(x[...].astype(F32), gain[...], grad_h)
    grad_x[...] = grad_r[...] + pulled
    sums[0:1, :] += gains
    sums[1:2, :] += shifts


def first_back(place, x, grad_r, gain, parts, pieces, after=()):
    count, width = x.shape
    block = 256
    return kernel_call(
        first_back_kernel,
        [place, x, grad_r, gain, *parts, *pieces],
        after,
        grid=(count // block,),
        in_specs=[SMEM, rows(block, width), rows(block, width), whole((1, width))]
        + [rows(block, part.shape[1]) for part in parts]
        + [HBM] * len(pieces),
        out_specs=[rows(block, width), whole((4, width))],
        out_shape=[jax.ShapeDtypeStruct((count, width), F32), jax.ShapeDtypeStruct((4, width), F32)],
        scratch_shapes=[pltpu.VMEM((width, 3 * width), BF16), pltpu.SemaphoreType.DMA],
        compiler_params=params(56),
        cost_estimate=cost(6 * count * width * width, 16e6),
        name="first_back",
    )


def pack_kernel(*refs):
    vectors, out = refs[:-1], refs[-1]
    devices, lanes = out.shape
    width = vectors[0].shape[1]
    unit = lanes // 12
    rows_of = [
        vector[row : row + 1, first : first + width]
        for vector in vectors
        for row in range(vector.shape[0])
        for first in range(0, vector.shape[1], width)
    ]
    total = jnp.zeros((devices, 12 * unit + (-12 * unit) % 128), F32)
    full = total.shape[1]
    at, base = 0, 0
    for span in (1, 1, 2, 1, 1, 1, 4, 1):
        size = span * unit + (-span * unit) % 128
        shape = (size, width)
        spreads = []
        for index in range(span):
            mine = owner((devices, width), span * unit, index * width)
            spreads.append(jnp.where(mine, rows_of[at + index], 0.0))
        at += span
        found = jnp.zeros((devices, size), F32)
        for index, spread in enumerate(spreads):
            pick = one_hot(shape, 0, span * unit, index * width).astype(BF16)
            high = spread.astype(BF16)
            low = (spread - high.astype(F32)).astype(BF16)
            both = dot(jnp.concatenate([high, low], 0), pick, NT)
            found = found + both[:devices] + both[devices:]
        if size < full:
            found = jnp.concatenate([found, jnp.zeros((devices, full - size), F32)], 1)
        total = total + (found if base == 0 else pltpu.roll(found, base * unit, 1))
        base += span
    out[...] = total[:, :lanes]


def pack(vectors, devices):
    lanes = sum(v.size for v in vectors) // devices
    return pl.pallas_call(
        pack_kernel,
        out_shape=jax.ShapeDtypeStruct((devices, lanes), F32),
        compiler_params=params(16),
        name="pack",
    )(*vectors)


def staged(
    tokens,
    doc_ids,
    d_out,
    ln1_gain,
    ln1_shift,
    qkv_weight,
    qv_bias,
    out_weight,
    out_bias,
    ln2_gain,
    ln2_shift,
    fc_weight,
    fc_bias,
    proj_weight,
    proj_bias,
):
    width = tokens.shape[1]
    depth = fc_weight.shape[1]
    devices = lax.axis_size("dp") * lax.axis_size("fsdp")
    index = lax.axis_index("dp") * lax.axis_size("fsdp") + lax.axis_index("fsdp")
    core = index & 1
    place = jnp.stack([index >> 1, core]).astype(jnp.int32)
    by_stage = (lax.axis_size("dp"), lax.axis_size("fsdp")) == (8, 4)

    smalls = [ln1_gain, ln1_shift, qv_bias, out_bias, ln2_gain, ln2_shift, fc_bias, proj_bias]
    smalls = jnp.concatenate([v.astype(F32).reshape(1, -1) for v in smalls], 1).reshape(-1)
    if by_stage:
        extra = jnp.pad(smalls, (0, -smalls.size % 128)).reshape(-1, 128).astype(BF16)
        extra = jnp.pad(extra, ((0, qkv_weight.shape[0] - extra.shape[0]), (0, 0)))
        first_block = pair_block(qkv_weight, core, extra)
        out_weight, fc_weight, proj_weight = tie([out_weight, fc_weight, proj_weight], first_block)
        wide_block = jnp.concatenate([pair_block(out_weight, core), pair_block(fc_weight, core)], 1)
        proj_block = pair_block(proj_weight, core)
        first_column = jnp.stack([first_block] + by_z([first_block] * 3))
        (wide_block,) = tie([wide_block], first_column)
        first_got, wide_got, (proj_near,) = meet(
            by_xy([first_column] * 3), by_z([wide_block] * 3), [swap(tie([proj_block], first_column)[0], Z0)]
        )
        first_pieces = gather_core([first_column, *first_got])
        wide_column = jnp.stack([wide_block] + wide_got)
        wide_got = by_xy([wide_column] * 3)
        (proj_block,) = tie([proj_block], wide_column)
        proj_got = [swap(proj_block, bits) for bits in (Z1, Z0 | Z1)]
    else:
        first_pieces, proj_pieces = [gather_all(qkv_weight)], [gather_all(proj_weight)]
        wide_pieces = [gather_all(w) for w in (out_weight, fc_weight)]
        wide_column = None
        table = gather_all(smalls.reshape(1, -1).astype(BF16))
        first_pieces = first_pieces + [jnp.pad(table, ((0, 0), (0, -table.shape[1] % 128)))]
    hold = lambda *some: list(some) if by_stage else []
    row = lambda at, count=1: vectors[at : at + count].reshape(1, -1)

    found = project_attend(place, tokens, doc_ids, first_pieces, after=hold(wide_column) if by_stage else [])
    if by_stage:
        found, wide_got, proj_got = meet(found, wide_got, proj_got)
        proj_column = jnp.stack([proj_block, proj_near] + proj_got)
        proj_got = by_xy([proj_column] * 3)
        wide_pieces = gather_core([wide_column, *wide_got])
    mixed, h_one, attended, lse, vectors = found

    found = widen(
        place,
        tokens,
        attended,
        row(4),
        row(5),
        row(6),
        row(7, 4),
        d_out,
        wide_pieces,
        after=hold(proj_column) if by_stage else [],
    )
    if by_stage:
        found, proj_got = meet(found, proj_got)
        proj_pieces = gather_core([proj_column, *proj_got])
        proj_sums = scatter_core(found[4:])
        proj_got = by_xy(proj_sums[1:])
    resid, h_two, slope, active, *proj_terms = found

    found = narrow(
        place,
        resid,
        active,
        slope,
        d_out,
        row(11),
        row(5),
        h_two,
        attended,
        wide_pieces,
        proj_pieces,
        after=hold(*proj_sums) if by_stage else [],
    )
    if by_stage:
        found, proj_got = meet(found, proj_got)
        proj_sums = sum_xy(proj_sums, proj_got)
        proj_got = by_z(proj_sums[1:])
        wide_sums = scatter_core(found[8:])
        wide_got = by_xy(wide_sums[1:])
    result, grad_r, grad_o, fc_sum, proj_sum, gain_two, shift_two, out_sum, *wide_terms = found

    found = attend_back(
        place,
        mixed,
        attended,
        grad_o,
        lse,
        doc_ids,
        h_one,
        by_stage,
        after=hold(*proj_sums, *wide_sums) if by_stage else [],
    )
    if by_stage:
        found, wide_got, proj_got = meet(found, wide_got, proj_got)
        wide_sums = sum_xy(wide_sums, wide_got)
        wide_got = by_z(wide_sums[1:])
        qkv_sums = scatter_core(found[3:])
        qkv_got = by_xy(qkv_sums[1:])
    *grads, qkv_terms = found[:4]

    found = first_back(
        place,
        tokens,
        grad_r,
        row(0),
        grads,
        first_pieces[:8] if by_stage else first_pieces[:1],
        after=hold(*qkv_sums, *wide_sums) if by_stage else [],
    )
    if by_stage:
        found, wide_got, qkv_got = meet(found, wide_got, qkv_got)
    grad_x, first_sums = found
    sums = [first_sums, out_sum, gain_two, shift_two, fc_sum, proj_sum]
    table = pack(sums, devices)
    if by_stage:
        qkv_sums = sum_xy(qkv_sums, qkv_got)
        table = scatter_small(tie([table], *qkv_sums)[0], index, (Z1, Z0, Y, X))
        (table,), qkv_got = meet([table], by_z(qkv_sums[1:]))
        proj_grad, wide_grad = add(proj_sums[0], *proj_got), add(wide_sums[0], *wide_got)
    else:
        own = scatter_all(table).reshape(-1)
        proj_grad, wide_grad, qkv_grad = (
            scatter_all(terms.astype(F32)) for terms in (proj_terms[0], wide_terms[0], qkv_terms)
        )

    def sides(grad):
        if by_stage:
            return own_rows(grad, core)
        return jnp.split(grad, 2, 1)

    proj_grad = jnp.concatenate(sides(proj_grad), 1)
    both = sides(wide_grad)
    half = depth // 2
    fc_grad = jnp.concatenate([side[:, :half] for side in both], 1)
    out_grad = jnp.concatenate([side[:, half:] for side in both], 1)
    if by_stage:
        own = scatter_small(table, index, (CORE,)).reshape(-1)
        qkv_grad = add(qkv_sums[0], *qkv_got)
    both = sides(qkv_grad)
    qkv_grad = jnp.concatenate(
        [side[:, lane : lane + PAIR] for lane in range(0, both[0].shape[1], PAIR) for side in both], 1
    )
    n = width // devices
    spots = (0, n, 2 * n, 4 * n, 5 * n, 6 * n, 7 * n, 11 * n, 12 * n)
    s = [own[a:b] for a, b in zip(spots[:-1], spots[1:])]
    return (
        result,
        grad_x,
        s[0],
        s[1],
        qkv_grad,
        s[2],
        out_grad,
        s[3],
        s[4],
        s[5],
        fc_grad,
        s[6],
        proj_grad,
        s[7],
    )


def solution(mesh):
    every, block = P(AXES), P(AXES, None)
    ins = (block, every, block, every, every, block, every, block, every, every, every, block, every, block, every)
    outs = (block, block, every, every, block, every, block, every, every, every, block, every, block, every)
    return jax.shard_map(staged, mesh=mesh, in_specs=ins, out_specs=outs, check_vma=False)
```

profile of v0, /device:TPU:0, one launch (start us, length us, event | category | flops | bytes accessed | tf_op | source)
XLA Modules:
  0.0 262.2 jit_solution(14189150231178237153)
XLA Ops:
  0.7 0.9 concatenate.37
  1.6 0.9 broadcast_select_fusion.17
  3.0 0.9 collective-permute-done
  4.0 3.0 %collective-permute-start.4 = (bf16[48,1280]{1,0:T(8,128)(2,1)S(1)}, bf16[48,1280]{1,0:T(8,128)(2,1)S(1)}, u32[]{:S(2)}, u32[]{:S(2)}) collective-permute-start(bf16[48,1280]{1,0:T(8,128)(2,1)S(1)} %get-tuple-element.253), channel_id=1, source_target_pairs={{0,8},{1,9},{2,10},{3,11},{4,12},{5,13},{6,14},{7,15},{8,0},{9,1},... | collective-permute-start | bytes 368648 | tf_op jit(solution)/shard_map/ppermute | solution.py:54
  7.0 2.6 collective-permute-start.5
  9.6 0.9 broadcast_select_fusion.10
  10.6 0.7 broadcast_select_fusion.20
  11.8 0.9 broadcast_select_fusion.4
  13.0 0.7 broadcast_select_fusion.19
  14.2 5.2 %collective-permute-done.5 = bf16[48,1280]{1,0:T(8,128)(2,1)S(1)} collective-permute-done((bf16[48,1280]{1,0:T(8,128)(2,1)S(1)}, bf16[48,1280]{1,0:T(8,128)(2,1)S(1)}, u32[]{:S(2)}, u32[]{:S(2)}) %collective-permute-start.5) | collective-permute-done | bytes 122912 | tf_op jit(solution)/shard_map/ppermute | solution.py:54
  19.4 1.6 collective-permute-start.7
  21.0 1.5 collective-permute-start.8
  23.0 2.2 collective-permute-start.10
  25.3 6.2 %collective-permute-done.13 = bf16[192,384]{1,0:T(8,128)(2,1)} collective-permute-done((bf16[192,384]{1,0:T(8,128)(2,1)S(1)}, bf16[192,384]{1,0:T(8,128)(2,1)}, u32[]{:S(2)}, u32[]{:S(2)}) %collective-permute-start.13) | collective-permute-done | bytes 147488 | tf_op jit(solution)/shard_map/ppermute | solution.py:54
  31.5 2.8 %collective-permute-start.11 = (bf16[48,1920]{1,0:T(8,128)(2,1)S(1)}, bf16[48,1920]{1,0:T(8,128)(2,1)S(1)}, u32[]{:S(2)}, u32[]{:S(2)}) collective-permute-start(bf16[48,1920]{1,0:T(8,128)(2,1)S(1)} %maximum_maximum_fusion), channel_id=1, source_target_pairs={{0,16},{1,17},{2,18},{3,19},{4,20},{5,21},{6,22},{7,23},{8,24},{9,... | collective-permute-start | bytes 552968 | tf_op jit(solution)/shard_map/ppermute | solution.py:54
  34.3 1.3 collective-permute-start.12
  35.6 10.0 %collective-permute-done.11 = bf16[48,1920]{1,0:T(8,128)(2,1)S(1)} collective-permute-done((bf16[48,1920]{1,0:T(8,128)(2,1)S(1)}, bf16[48,1920]{1,0:T(8,128)(2,1)S(1)}, u32[]{:S(2)}, u32[]{:S(2)}) %collective-permute-start.11) | collective-permute-done | bytes 184352 | tf_op jit(solution)/shard_map/ppermute | solution.py:54
  47.1 1.3 pad_maximum_fusion.rest_0_
  48.5 3.9 %collective-permute-start.21 = (bf16[192,384]{1,0:T(8,128)(2,1)S(1)}, bf16[192,384]{1,0:T(8,128)(2,1)S(1)}, u32[]{:S(2)}, u32[]{:S(2)}) collective-permute-start(bf16[192,384]{1,0:T(8,128)(2,1)S(1)} %pad_maximum_fusion.5), channel_id=1, source_target_pairs={{0,16},{1,17},{2,18},{3,19},{4,20},{5,21},{6,22},{7,23},{8,24},{9,... | collective-permute-start | bytes 442376 | tf_op jit(solution)/shard_map/ppermute | solution.py:54
  52.4 1.3 collective-permute-start.22
  53.7 1.5 collective-permute-start.18
  55.2 1.5 collective-permute-start.19
  57.2 28.6 %project_attend.1 = (bf16[1024,2304]{1,0:T(8,128)(2,1)}, bf16[1024,768]{1,0:T(8,128)(2,1)}, bf16[1024,768]{1,0:T(8,128)(2,1)S(1)}, f32[6,2,1024]{2,1,0:T(2,128)S(1)}, f32[12,768]{1,0:T(8,128)S(1)}) custom-call(s32[2]{0:T(128)S(1)} %pad_add_fusion.place, bf16[1024,768]{1,0:T(8,128)(2,1)S(1)} %copy-done.5, s32[1024,1]{1,0:T(8,128)S(1)} %copy.29.q_docs.k_docs, ...), custom_call_target="tpu_custom_call" | custom-call | flops 28000000000 | bytes 20000000 | tf_op jit(solution)/shard_map/project_attend/pallas_call | solution.py:111
  86.5 2.5 collective-permute-done.19.rest_2_
  89.6 1.0 pad_maximum_fusion.1.rest_8_
  90.6 1.3 collective-permute-start.27
  92.5 0.8 collective-permute-start.28
  93.3 1.4 collective-permute-start.29
  94.8 24.3 %widen.1 = (f32[1024,768]{1,0:T(8,128)}, bf16[1024,768]{1,0:T(8,128)(2,1)S(1)}, bf16[1024,3072]{1,0:T(8,128)(2,1)}, bf16[1024,3072]{1,0:T(8,128)(2,1)}, bf16[4,4...) custom-call(s32[2]{0:T(128)S(1)} %pad_add_fusion.place, bf16[1024,768]{1,0:T(8,128)(2,1)S(1)} %copy-done.5, ...), custom_call_target="tpu_custom_call" | custom-call | flops 10871635968 | bytes 30000000 | tf_op jit(solution)/shard_map/widen/pallas_call | solution.py:111
  119.1 1.4 collective-permute-done.28.rest_10_
  121.6 3.5 %collective-permute-done.30 = bf16[4,4,192,384]{3,2,1,0:T(8,128)(2,1)S(1)} collective-permute-done((bf16[4,4,192,384]{3,2,1,0:T(8,128)(2,1)S(1)}, bf16[4,4,192,384]{3,2,1,0:T(8,128)(2,1)S(1)}, u32[]{:S(2)}, u32[]{:S(2)}) %collective-permute-start.30) | collective-permute-done | bytes 2359328 | tf_op jit(solution)/shard_map/ppermute | solution.py:54
  125.8 0.9 collective-permute-start.35
  126.7 1.5 collective-permute-start.36
  128.2 1.2 collective-permute-start.37
  129.4 33.8 %narrow.1 = (bf16[1024,768]{1,0:T(8,128)(2,1)}, f32[1024,768]{1,0:T(8,128)}, bf16[1024,768]{1,0:T(8,128)(2,1)S(1)}, f32[1,3072]{1,0:T(1,128)S(1)}, f32[1,768]{1,...) custom-call(s32[2]{0:T(128)S(1)} %pad_add_fusion.place, ...), custom_call_target="tpu_custom_call" | custom-call | flops 21743271936 | bytes 40000000 | tf_op jit(solution)/shard_map/narrow/pallas_call | solution.py:111
  163.7 3.0 %collective-permute-start.43 = (bf16[192,384]{1,0:T(8,128)(2,1)S(1)}, bf16[192,384]{1,0:T(8,128)(2,1)S(1)}, u32[]{:S(2)}, u32[]{:S(2)}) collective-permute-start(bf16[192,384]{1,0:T(8,128)(2,1)S(1)} %get-tuple-element.235), channel_id=1, source_target_pairs={{0,16},{1,17},{2,18},{3,19},{4,20},{5,21},{6,22},{7,23},{8,24},{9,... | collective-permute-start | bytes 442376 | tf_op jit(solution)/shard_map/ppermute | solution.py:54
  166.8 1.3 collective-permute-start.44
  168.1 0.8 collective-permute-done.38
  169.6 0.9 collective-permute-start.39
  170.5 1.5 collective-permute-start.40
  172.0 0.9 collective-permute-done.42
  172.9 1.7 collective-permute-start.41
  174.7 34.3 %attend_back.1 = (bf16[1024,768]{1,0:T(8,128)(2,1)}, bf16[1024,768]{1,0:T(8,128)(2,1)}, bf16[1024,768]{1,0:T(8,128)(2,1)}, bf16[4,4,48,1152]{3,2,1,0:T(8,128)(2,1)}, bf16[4,4,48,1152]{3,2,1,0:T(8,128)(2,1)}) custom-call(s32[2]{0:T(128)} %copy-done.7, s32[1,1024]{1,0:T(1,128)} %bitcast.150, s32[1024,1]{1,0:T(8,128)} %copy-done, ...), custom_call_target="tpu_custom_call" | custom-call | flops 41999998976 | bytes 20000000 | tf_op jit(solution)/shard_map/attend_back/pallas_call | solution.py:111
  209.0 0.9 copy-done.14
  210.2 2.0 fusion.48
  212.3 1.0 convert_add_fusion.9
  213.3 0.8 collective-permute-done.45
  215.2 1.2 collective-permute-start.50
  216.4 1.7 collective-permute-start.51
  218.2 1.2 collective-permute-start.47
  219.4 2.4 collective-permute-start.48
  221.8 11.3 %first_back.1 = (f32[1024,768]{1,0:T(8,128)}, f32[4,768]{1,0:T(4,128)}) custom-call(s32[2]{0:T(128)} %copy-done.7, bf16[1024,768]{1,0:T(8,128)(2,1)} %x.9, f32[1024,768]{1,0:T(8,128)} %get-tuple-element.191.grad_r, f32[1,768]{1,0:T(1,128)} %get-tuple-element.260.gain, bf16[1024,768]{1,0:T(8,128)(2,1)} %get-tuple-element.192.rest_0_, ...), custom_call_target="tpu_custom_call" | custom-call | flops 3623878656 | bytes 16000000 | tf_op jit(solution)/shard_map/first_back/pallas_call | solution.py:111
  233.7 2.9 %collective-permute-done.50 = bf16[4,48,1152]{2,1,0:T(8,128)(2,1)S(1)} collective-permute-done((bf16[4,48,1152]{2,1,0:T(8,128)(2,1)S(1)}, bf16[4,48,1152]{2,1,0:T(8,128)(2,1)S(1)}, u32[]{:S(2)}, u32[]{:S(2)}) %collective-permute-start.50) | collective-permute-done | bytes 442400 | tf_op jit(solution)/shard_map/ppermute | solution.py:54
  236.9 1.0 pack.1
  237.9 1.3 collective-permute-start.52
  239.3 3.4 %collective-permute-done.52 = f32[16,288]{1,0:T(8,128)S(1)} collective-permute-done((f32[16,288]{1,0:T(8,128)S(1)}, f32[16,288]{1,0:T(8,128)S(1)}, u32[]{:S(2)}, u32[]{:S(2)}) %collective-permute-start.52) | collective-permute-done | bytes 18464 | tf_op jit(solution)/shard_map/ppermute | solution.py:54
  242.7 1.3 collective-permute-start.53
  244.8 0.8 collective-permute-start.56
  245.5 1.3 collective-permute-start.57
  246.8 2.4 collective-permute-start.58
  249.2 1.3 collective-permute-start.54
  250.5 2.3 collective-permute-done.54
  252.9 1.6 collective-permute-start.55
  254.5 2.0 collective-permute-done.55
  (196 shorter events, 17.6 us)
Async XLA Ops:
  2.5 1.4 collective-permute-start
  4.0 10.2 %collective-permute-start.4 = (bf16[48,1280]{1,0:T(8,128)(2,1)S(1)}, bf16[48,1280]{1,0:T(8,128)(2,1)S(1)}, u32[]{:S(2)}, u32[]{:S(2)}) collective-permute-start(bf16[48,1280]{1,0:T(8,128)(2,1)S(1)} %get-tuple-element.253), channel_id=1, source_target_pairs={{0,8},{1,9},{2,10},{3,11},{4,12},{5,13},{6,14},{7,15},{8,0},{9,1},... | collective-permute-start | bytes 368648 | tf_op jit(solution)/shard_map/ppermute | solution.py:54
  7.0 12.4 %collective-permute-start.5 = (bf16[48,1280]{1,0:T(8,128)(2,1)S(1)}, bf16[48,1280]{1,0:T(8,128)(2,1)S(1)}, u32[]{:S(2)}, u32[]{:S(2)}) collective-permute-start(bf16[48,1280]{1,0:T(8,128)(2,1)S(1)} %get-tuple-element.253), channel_id=1, source_target_pairs={{0,16},{1,17},{2,18},{3,19},{4,20},{5,21},{6,22},{7,23},{8,24},{9,... | collective-permute-start | bytes 368648 | tf_op jit(solution)/shard_map/ppermute | solution.py:54
  9.6 9.8 %collective-permute-start.6 = (bf16[48,1280]{1,0:T(8,128)(2,1)S(1)}, bf16[48,1280]{1,0:T(8,128)(2,1)S(1)}, u32[]{:S(2)}, u32[]{:S(2)}) collective-permute-start(bf16[48,1280]{1,0:T(8,128)(2,1)S(1)} %get-tuple-element.253), channel_id=1, source_target_pairs={{0,24},{1,25},{2,26},{3,27},{4,28},{5,29},{6,30},{7,31},{8,16},{9,... | collective-permute-start | bytes 368648 | tf_op jit(solution)/shard_map/ppermute | solution.py:54
  10.5 3.6 %collective-permute-start.1 = (bf16[96,384]{1,0:T(8,128)(2,1)S(1)}, bf16[96,384]{1,0:T(8,128)(2,1)S(1)}, u32[]{:S(2)}, u32[]{:S(2)}) collective-permute-start(bf16[96,384]{1,0:T(8,128)(2,1)S(1)} %broadcast_select_fusion.10), channel_id=1, source_target_pairs={{0,1},{1,0},{2,3},{3,2},{4,5},{5,4},{6,7},{7,6},{8,9},{9,8},{10,11... | collective-permute-start | bytes 221192 | tf_op jit(solution)/shard_map/ppermute | solution.py:54
  11.3 1.4 collective-permute-start.2
  12.8 1.3 collective-permute-start.3
  19.4 26.2 %collective-permute-start.7 = (bf16[4,48,1280]{2,1,0:T(8,128)(2,1)S(1)}, bf16[4,48,1280]{2,1,0:T(8,128)(2,1)S(1)}, u32[]{:S(2)}, u32[]{:S(2)}) collective-permute-start(bf16[4,48,1280]{2,1,0:T(8,128)(2,1)S(1)} %pad_maximum_fusion.2.rest_0_.rest_3_), channel_id=1, source_target_pairs={{0,2},{1,3},{2,0},{3,1},{4,6},{5,7},{6,4},{7,5},{8,10},{9,11},{10,... | collective-permute-start | bytes 1474568 | tf_op jit(solution)/shard_map/ppermute | solution.py:54
  21.0 24.7 %collective-permute-start.8 = (bf16[4,48,1280]{2,1,0:T(8,128)(2,1)S(1)}, bf16[4,48,1280]{2,1,0:T(8,128)(2,1)}, u32[]{:S(2)}, u32[]{:S(2)}) collective-permute-start(bf16[4,48,1280]{2,1,0:T(8,128)(2,1)S(1)} %pad_maximum_fusion.2.rest_0_.rest_3_), channel_id=1, source_target_pairs={{0,4},{1,5},{2,6},{3,7},{4,0},{5,1},{6,2},{7,3},{8,12},{9,13},{10,... | collective-permute-start | bytes 1474568 | tf_op jit(solution)/shard_map/ppermute | solution.py:54
  22.5 23.2 %collective-permute-start.9 = (bf16[4,48,1280]{2,1,0:T(8,128)(2,1)S(1)}, bf16[4,48,1280]{2,1,0:T(8,128)(2,1)}, u32[]{:S(2)}, u32[]{:S(2)}) collective-permute-start(bf16[4,48,1280]{2,1,0:T(8,128)(2,1)S(1)} %pad_maximum_fusion.2.rest_0_.rest_3_), channel_id=1, source_target_pairs={{0,6},{1,7},{2,4},{3,5},{4,2},{5,3},{6,0},{7,1},{8,14},{9,15},{10,... | collective-permute-start | bytes 1474568 | tf_op jit(solution)/shard_map/ppermute | solution.py:54
  23.0 11.3 %collective-permute-start.10 = (bf16[48,1920]{1,0:T(8,128)(2,1)S(1)}, bf16[48,1920]{1,0:T(8,128)(2,1)S(1)}, u32[]{:S(2)}, u32[]{:S(2)}) collective-permute-start(bf16[48,1920]{1,0:T(8,128)(2,1)S(1)} %maximum_maximum_fusion), channel_id=1, source_target_pairs={{0,8},{1,9},{2,10},{3,11},{4,12},{5,13},{6,14},{7,15},{8,0},{9,1},... | collective-permute-start | bytes 552968 | tf_op jit(solution)/shard_map/ppermute | solution.py:54
  25.2 6.3 %collective-permute-start.13 = (bf16[192,384]{1,0:T(8,128)(2,1)S(1)}, bf16[192,384]{1,0:T(8,128)(2,1)}, u32[]{:S(2)}, u32[]{:S(2)}) collective-permute-start(bf16[192,384]{1,0:T(8,128)(2,1)S(1)} %pad_maximum_fusion.5), channel_id=1, source_target_pairs={{0,8},{1,9},{2,10},{3,11},{4,12},{5,13},{6,14},{7,15},{8,0},{9,1},... | collective-permute-start | bytes 442376 | tf_op jit(solution)/shard_map/ppermute | solution.py:54
  31.5 14.1 %collective-permute-start.11 = (bf16[48,1920]{1,0:T(8,128)(2,1)S(1)}, bf16[48,1920]{1,0:T(8,128)(2,1)S(1)}, u32[]{:S(2)}, u32[]{:S(2)}) collective-permute-start(bf16[48,1920]{1,0:T(8,128)(2,1)S(1)} %maximum_maximum_fusion), channel_id=1, source_target_pairs={{0,16},{1,17},{2,18},{3,19},{4,20},{5,21},{6,22},{7,23},{8,24},{9,... | collective-permute-start | bytes 552968 | tf_op jit(solution)/shard_map/ppermute | solution.py:54
  34.3 11.3 %collective-permute-start.12 = (bf16[48,1920]{1,0:T(8,128)(2,1)S(1)}, bf16[48,1920]{1,0:T(8,128)(2,1)S(1)}, u32[]{:S(2)}, u32[]{:S(2)}) collective-permute-start(bf16[48,1920]{1,0:T(8,128)(2,1)S(1)} %maximum_maximum_fusion), channel_id=1, source_target_pairs={{0,24},{1,25},{2,26},{3,27},{4,28},{5,29},{6,30},{7,31},{8,16},{9,... | collective-permute-start | bytes 552968 | tf_op jit(solution)/shard_map/ppermute | solution.py:54
  45.6 6.8 %collective-permute-start.14 = (bf16[4,48,1280]{2,1,0:T(8,128)(2,1)S(1)}, bf16[4,48,1280]{2,1,0:T(8,128)(2,1)}, u32[]{:S(2)}, u32[]{:S(2)}) collective-permute-start(bf16[4,48,1280]{2,1,0:T(8,128)(2,1)S(1)} %pad_maximum_fusion.2.rest_0_.rest_3_), channel_id=1, source_target_pairs={{0,1},{1,0},{2,3},{3,2},{4,5},{5,4},{6,7},{7,6},{8,9},{9,8},{10,11... | collective-permute-start | bytes 1474568 | tf_op jit(solution)/shard_map/ppermute | solution.py:54
  45.7 8.0 %collective-permute-start.15 = (bf16[4,48,1280]{2,1,0:T(8,128)(2,1)S(1)}, bf16[4,48,1280]{2,1,0:T(8,128)(2,1)}, u32[]{:S(2)}, u32[]{:S(2)}) collective-permute-start(bf16[4,48,1280]{2,1,0:T(8,128)(2,1)S(1)} %collective-permute-done.7.rest_1_.rest_4_), channel_id=1, source_target_pairs={{0,1},{1,0},{2,3},{3,2},{4,5},{5,4},{6,7},{7,6},{8,9},{9,8},{10,11... | collective-permute-start | bytes 1474568 | tf_op jit(solution)/shard_map/ppermute | solution.py:54
  46.3 8.9 %collective-permute-start.16 = (bf16[4,48,1280]{2,1,0:T(8,128)(2,1)}, bf16[4,48,1280]{2,1,0:T(8,128)(2,1)}, u32[]{:S(2)}, u32[]{:S(2)}) collective-permute-start(bf16[4,48,1280]{2,1,0:T(8,128)(2,1)} %collective-permute-done.8.rest_2_.rest_5_), channel_id=1, source_target_pairs={{0,1},{1,0},{2,3},{3,2},{4,5},{5,4},{6,7},{7,6},{8,9},{9,8},{10,11... | collective-permute-start | bytes 1474568 | tf_op jit(solution)/shard_map/ppermute | solution.py:54
  46.3 10.4 %collective-permute-start.17 = (bf16[4,48,1280]{2,1,0:T(8,128)(2,1)}, bf16[4,48,1280]{2,1,0:T(8,128)(2,1)}, u32[]{:S(2)}, u32[]{:S(2)}) collective-permute-start(bf16[4,48,1280]{2,1,0:T(8,128)(2,1)} %collective-permute-done.9.rest_3_.rest_6_), channel_id=1, source_target_pairs={{0,1},{1,0},{2,3},{3,2},{4,5},{5,4},{6,7},{7,6},{8,9},{9,8},{10,11... | collective-permute-start | bytes 1474568 | tf_op jit(solution)/shard_map/ppermute | solution.py:54
  47.1 82.3 %copy-start.7 = (s32[2]{0:T(128)}, s32[2]{0:T(128)S(1)}, u32[]{:S(2)}) copy-start(s32[2]{0:T(128)S(1)} %pad_add_fusion.place) | copy-start | bytes 28
  48.5 38.1 %collective-permute-start.21 = (bf16[192,384]{1,0:T(8,128)(2,1)S(1)}, bf16[192,384]{1,0:T(8,128)(2,1)S(1)}, u32[]{:S(2)}, u32[]{:S(2)}) collective-permute-start(bf16[192,384]{1,0:T(8,128)(2,1)S(1)} %pad_maximum_fusion.5), channel_id=1, source_target_pairs={{0,16},{1,17},{2,18},{3,19},{4,20},{5,21},{6,22},{7,23},{8,24},{9,... | collective-permute-start | bytes 442376 | tf_op jit(solution)/shard_map/ppermute | solution.py:54
  52.4 34.1 %collective-permute-start.22 = (bf16[192,384]{1,0:T(8,128)(2,1)S(1)}, bf16[192,384]{1,0:T(8,128)(2,1)S(1)}, u32[]{:S(2)}, u32[]{:S(2)}) collective-permute-start(bf16[192,384]{1,0:T(8,128)(2,1)S(1)} %pad_maximum_fusion.5), channel_id=1, source_target_pairs={{0,24},{1,25},{2,26},{3,27},{4,28},{5,29},{6,30},{7,31},{8,16},{9,... | collective-permute-start | bytes 442376 | tf_op jit(solution)/shard_map/ppermute | solution.py:54
  53.7 32.8 %collective-permute-start.18 = (bf16[4,48,1920]{2,1,0:T(8,128)(2,1)S(1)}, bf16[4,48,1920]{2,1,0:T(8,128)(2,1)S(1)}, u32[]{:S(2)}, u32[]{:S(2)}) collective-permute-start(bf16[4,48,1920]{2,1,0:T(8,128)(2,1)S(1)} %pad_maximum_fusion.rest_0_), channel_id=1, source_target_pairs={{0,2},{1,3},{2,0},{3,1},{4,6},{5,7},{6,4},{7,5},{8,10},{9,11},{10,... | collective-permute-start | bytes 2211848 | tf_op jit(solution)/shard_map/ppermute | solution.py:54
  55.2 33.8 %collective-permute-start.19 = (bf16[4,48,1920]{2,1,0:T(8,128)(2,1)S(1)}, bf16[4,48,1920]{2,1,0:T(8,128)(2,1)S(1)}, u32[]{:S(2)}, u32[]{:S(2)}) collective-permute-start(bf16[4,48,1920]{2,1,0:T(8,128)(2,1)S(1)} %pad_maximum_fusion.rest_0_), channel_id=1, source_target_pairs={{0,4},{1,5},{2,6},{3,7},{4,0},{5,1},{6,2},{7,3},{8,12},{9,13},{10,... | collective-permute-start | bytes 2211848 | tf_op jit(solution)/shard_map/ppermute | solution.py:54
  56.7 32.3 %collective-permute-start.20 = (bf16[4,48,1920]{2,1,0:T(8,128)(2,1)S(1)}, bf16[4,48,1920]{2,1,0:T(8,128)(2,1)S(1)}, u32[]{:S(2)}, u32[]{:S(2)}) collective-permute-start(bf16[4,48,1920]{2,1,0:T(8,128)(2,1)S(1)} %pad_maximum_fusion.rest_0_), channel_id=1, source_target_pairs={{0,6},{1,7},{2,4},{3,5},{4,2},{5,3},{6,0},{7,1},{8,14},{9,15},{10,... | collective-permute-start | bytes 2211848 | tf_op jit(solution)/shard_map/ppermute | solution.py:54
  86.5 6.0 %collective-permute-start.23 = (bf16[4,48,1920]{2,1,0:T(8,128)(2,1)S(1)}, bf16[4,48,1920]{2,1,0:T(8,128)(2,1)S(1)}, u32[]{:S(2)}, u32[]{:S(2)}) collective-permute-start(bf16[4,48,1920]{2,1,0:T(8,128)(2,1)S(1)} %pad_maximum_fusion.rest_0_), channel_id=1, source_target_pairs={{0,1},{1,0},{2,3},{3,2},{4,5},{5,4},{6,7},{7,6},{8,9},{9,8},{10,11... | collective-permute-start | bytes 2211848 | tf_op jit(solution)/shard_map/ppermute | solution.py:54
  89.1 4.3 %collective-permute-start.24 = (bf16[4,48,1920]{2,1,0:T(8,128)(2,1)S(1)}, bf16[4,48,1920]{2,1,0:T(8,128)(2,1)S(1)}, u32[]{:S(2)}, u32[]{:S(2)}) collective-permute-start(bf16[4,48,1920]{2,1,0:T(8,128)(2,1)S(1)} %collective-permute-done.18.rest_1_), channel_id=1, source_target_pairs={{0,1},{1,0},{2,3},{3,2},{4,5},{5,4},{6,7},{7,6},{8,9},{9,8},{10,11... | collective-permute-start | bytes 2211848 | tf_op jit(solution)/shard_map/ppermute | solution.py:54
  89.1 5.7 %collective-permute-start.25 = (bf16[4,48,1920]{2,1,0:T(8,128)(2,1)S(1)}, bf16[4,48,1920]{2,1,0:T(8,128)(2,1)S(1)}, u32[]{:S(2)}, u32[]{:S(2)}) collective-permute-start(bf16[4,48,1920]{2,1,0:T(8,128)(2,1)S(1)} %collective-permute-done.19.rest_2_), channel_id=1, source_target_pairs={{0,1},{1,0},{2,3},{3,2},{4,5},{5,4},{6,7},{7,6},{8,9},{9,8},{10,11... | collective-permute-start | bytes 2211848 | tf_op jit(solution)/shard_map/ppermute | solution.py:54
  89.6 5.2 %collective-permute-start.26 = (bf16[4,48,1920]{2,1,0:T(8,128)(2,1)S(1)}, bf16[4,48,1920]{2,1,0:T(8,128)(2,1)S(1)}, u32[]{:S(2)}, u32[]{:S(2)}) collective-permute-start(bf16[4,48,1920]{2,1,0:T(8,128)(2,1)S(1)} %collective-permute-done.20.rest_3_), channel_id=1, source_target_pairs={{0,1},{1,0},{2,3},{3,2},{4,5},{5,4},{6,7},{7,6},{8,9},{9,8},{10,11... | collective-permute-start | bytes 2211848 | tf_op jit(solution)/shard_map/ppermute | solution.py:54
  90.6 28.6 %collective-permute-start.27 = (bf16[4,192,384]{2,1,0:T(8,128)(2,1)S(1)}, bf16[4,192,384]{2,1,0:T(8,128)(2,1)S(1)}, u32[]{:S(2)}, u32[]{:S(2)}) collective-permute-start(bf16[4,192,384]{2,1,0:T(8,128)(2,1)S(1)} %pad_maximum_fusion.1.rest_8_), channel_id=1, source_target_pairs={{0,2},{1,3},{2,0},{3,1},{4,6},{5,7},{6,4},{7,5},{8,10},{9,11},{10,... | collective-permute-start | bytes 1769480 | tf_op jit(solution)/shard_map/ppermute | solution.py:54
  92.5 28.1 %collective-permute-start.28 = (bf16[4,192,384]{2,1,0:T(8,128)(2,1)S(1)}, bf16[4,192,384]{2,1,0:T(8,128)(2,1)S(1)}, u32[]{:S(2)}, u32[]{:S(2)}) collective-permute-start(bf16[4,192,384]{2,1,0:T(8,128)(2,1)S(1)} %pad_maximum_fusion.1.rest_8_), channel_id=1, source_target_pairs={{0,4},{1,5},{2,6},{3,7},{4,0},{5,1},{6,2},{7,3},{8,12},{9,13},{10,... | collective-permute-start | bytes 1769480 | tf_op jit(solution)/shard_map/ppermute | solution.py:54
  93.3 27.3 %collective-permute-start.29 = (bf16[4,192,384]{2,1,0:T(8,128)(2,1)S(1)}, bf16[4,192,384]{2,1,0:T(8,128)(2,1)S(1)}, u32[]{:S(2)}, u32[]{:S(2)}) collective-permute-start(bf16[4,192,384]{2,1,0:T(8,128)(2,1)S(1)} %pad_maximum_fusion.1.rest_8_), channel_id=1, source_target_pairs={{0,6},{1,7},{2,4},{3,5},{4,2},{5,3},{6,0},{7,1},{8,14},{9,15},{10,... | collective-permute-start | bytes 1769480 | tf_op jit(solution)/shard_map/ppermute | solution.py:54
  120.6 4.5 %collective-permute-start.30 = (bf16[4,4,192,384]{3,2,1,0:T(8,128)(2,1)S(1)}, bf16[4,4,192,384]{3,2,1,0:T(8,128)(2,1)S(1)}, u32[]{:S(2)}, u32[]{:S(2)}) collective-permute-start(bf16[4,4,192,384]{3,2,1,0:T(8,128)(2,1)S(1)} %get-tuple-element.150), channel_id=1, source_target_pairs={{0,1},{1,0},{2,3},{3,2},{4,5},{5,4},{6,7},{7,6},{8,9},{9,8},{10,11... | collective-permute-start | bytes 7077896 | tf_op jit(solution)/shard_map/ppermute | solution.py:54
  120.6 6.1 %collective-permute-start.31 = (bf16[4,192,384]{2,1,0:T(8,128)(2,1)S(1)}, bf16[4,192,384]{2,1,0:T(8,128)(2,1)S(1)}, u32[]{:S(2)}, u32[]{:S(2)}) collective-permute-start(bf16[4,192,384]{2,1,0:T(8,128)(2,1)S(1)} %pad_maximum_fusion.1.rest_8_), channel_id=1, source_target_pairs={{0,1},{1,0},{2,3},{3,2},{4,5},{5,4},{6,7},{7,6},{8,9},{9,8},{10,11... | collective-permute-start | bytes 1769480 | tf_op jit(solution)/shard_map/ppermute | solution.py:54
  121.1 7.1 %collective-permute-start.32 = (bf16[4,192,384]{2,1,0:T(8,128)(2,1)S(1)}, bf16[4,192,384]{2,1,0:T(8,128)(2,1)S(1)}, u32[]{:S(2)}, u32[]{:S(2)}) collective-permute-start(bf16[4,192,384]{2,1,0:T(8,128)(2,1)S(1)} %collective-permute-done.27.rest_9_), channel_id=1, source_target_pairs={{0,1},{1,0},{2,3},{3,2},{4,5},{5,4},{6,7},{7,6},{8,9},{9,8},{10,11... | collective-permute-start | bytes 1769480 | tf_op jit(solution)/shard_map/ppermute | solution.py:54
  121.1 8.3 %collective-permute-start.33 = (bf16[4,192,384]{2,1,0:T(8,128)(2,1)S(1)}, bf16[4,192,384]{2,1,0:T(8,128)(2,1)S(1)}, u32[]{:S(2)}, u32[]{:S(2)}) collective-permute-start(bf16[4,192,384]{2,1,0:T(8,128)(2,1)S(1)} %collective-permute-done.28.rest_10_), channel_id=1, source_target_pairs={{0,1},{1,0},{2,3},{3,2},{4,5},{5,4},{6,7},{7,6},{8,9},{9,8},{10,11... | collective-permute-start | bytes 1769480 | tf_op jit(solution)/shard_map/ppermute | solution.py:54
  121.6 7.8 %collective-permute-start.34 = (bf16[4,192,384]{2,1,0:T(8,128)(2,1)S(1)}, bf16[4,192,384]{2,1,0:T(8,128)(2,1)S(1)}, u32[]{:S(2)}, u32[]{:S(2)}) collective-permute-start(bf16[4,192,384]{2,1,0:T(8,128)(2,1)S(1)} %collective-permute-done.29.rest_11_), channel_id=1, source_target_pairs={{0,1},{1,0},{2,3},{3,2},{4,5},{5,4},{6,7},{7,6},{8,9},{9,8},{10,11... | collective-permute-start | bytes 1769480 | tf_op jit(solution)/shard_map/ppermute | solution.py:54
  125.8 37.4 %collective-permute-start.35 = (bf16[4,192,384]{2,1,0:T(8,128)(2,1)S(1)}, bf16[4,192,384]{2,1,0:T(8,128)(2,1)S(1)}, u32[]{:S(2)}, u32[]{:S(2)}) collective-permute-start(bf16[4,192,384]{2,1,0:T(8,128)(2,1)S(1)} %get-tuple-element.225), channel_id=1, source_target_pairs={{0,2},{1,3},{2,0},{3,1},{4,6},{5,7},{6,4},{7,5},{8,10},{9,11},{10,... | collective-permute-start | bytes 1769480 | tf_op jit(solution)/shard_map/ppermute | solution.py:54
  126.7 36.5 %collective-permute-start.36 = (bf16[4,192,384]{2,1,0:T(8,128)(2,1)S(1)}, bf16[4,192,384]{2,1,0:T(8,128)(2,1)S(1)}, u32[]{:S(2)}, u32[]{:S(2)}) collective-permute-start(bf16[4,192,384]{2,1,0:T(8,128)(2,1)S(1)} %get-tuple-element.224), channel_id=1, source_target_pairs={{0,4},{1,5},{2,6},{3,7},{4,0},{5,1},{6,2},{7,3},{8,12},{9,13},{10,... | collective-permute-start | bytes 1769480 | tf_op jit(solution)/shard_map/ppermute | solution.py:54
  128.2 35.0 %collective-permute-start.37 = (bf16[4,192,384]{2,1,0:T(8,128)(2,1)S(1)}, bf16[4,192,384]{2,1,0:T(8,128)(2,1)S(1)}, u32[]{:S(2)}, u32[]{:S(2)}) collective-permute-start(bf16[4,192,384]{2,1,0:T(8,128)(2,1)S(1)} %get-tuple-element.223), channel_id=1, source_target_pairs={{0,6},{1,7},{2,4},{3,5},{4,2},{5,3},{6,0},{7,1},{8,14},{9,15},{10,... | collective-permute-start | bytes 1769480 | tf_op jit(solution)/shard_map/ppermute | solution.py:54
  163.2 5.7 %collective-permute-start.38 = (bf16[4,4,48,1920]{3,2,1,0:T(8,128)(2,1)}, bf16[4,4,48,1920]{3,2,1,0:T(8,128)(2,1)S(1)}, u32[]{:S(2)}, u32[]{:S(2)}) collective-permute-start(bf16[4,4,48,1920]{3,2,1,0:T(8,128)(2,1)} %get-tuple-element.174), channel_id=1, source_target_pairs={{0,1},{1,0},{2,3},{3,2},{4,5},{5,4},{6,7},{7,6},{8,9},{9,8},{10,11... | collective-permute-start | bytes 8847368 | tf_op jit(solution)/shard_map/ppermute | solution.py:54
  163.6 9.3 %collective-permute-start.42 = (bf16[192,384]{1,0:T(8,128)(2,1)S(1)}, bf16[192,384]{1,0:T(8,128)(2,1)}, u32[]{:S(2)}, u32[]{:S(2)}) collective-permute-start(bf16[192,384]{1,0:T(8,128)(2,1)S(1)} %get-tuple-element.236), channel_id=1, source_target_pairs={{0,8},{1,9},{2,10},{3,11},{4,12},{5,13},{6,14},{7,15},{8,0},{9,1},... | collective-permute-start | bytes 442376 | tf_op jit(solution)/shard_map/ppermute | solution.py:54
  163.7 45.2 %collective-permute-start.43 = (bf16[192,384]{1,0:T(8,128)(2,1)S(1)}, bf16[192,384]{1,0:T(8,128)(2,1)S(1)}, u32[]{:S(2)}, u32[]{:S(2)}) collective-permute-start(bf16[192,384]{1,0:T(8,128)(2,1)S(1)} %get-tuple-element.235), channel_id=1, source_target_pairs={{0,16},{1,17},{2,18},{3,19},{4,20},{5,21},{6,22},{7,23},{8,24},{9,... | collective-permute-start | bytes 442376 | tf_op jit(solution)/shard_map/ppermute | solution.py:54
  166.8 42.2 %collective-permute-start.44 = (bf16[192,384]{1,0:T(8,128)(2,1)S(1)}, bf16[192,384]{1,0:T(8,128)(2,1)S(1)}, u32[]{:S(2)}, u32[]{:S(2)}) collective-permute-start(bf16[192,384]{1,0:T(8,128)(2,1)S(1)} %get-tuple-element.234), channel_id=1, source_target_pairs={{0,24},{1,25},{2,26},{3,27},{4,28},{5,29},{6,30},{7,31},{8,16},{9,... | collective-permute-start | bytes 442376 | tf_op jit(solution)/shard_map/ppermute | solution.py:54
  169.6 39.3 %collective-permute-start.39 = (bf16[4,48,1920]{2,1,0:T(8,128)(2,1)S(1)}, bf16[4,48,1920]{2,1,0:T(8,128)(2,1)S(1)}, u32[]{:S(2)}, u32[]{:S(2)}) collective-permute-start(bf16[4,48,1920]{2,1,0:T(8,128)(2,1)S(1)} %get-tuple-element.221), channel_id=1, source_target_pairs={{0,2},{1,3},{2,0},{3,1},{4,6},{5,7},{6,4},{7,5},{8,10},{9,11},{10,... | collective-permute-start | bytes 2211848 | tf_op jit(solution)/shard_map/ppermute | solution.py:54
  170.5 38.5 %collective-permute-start.40 = (bf16[4,48,1920]{2,1,0:T(8,128)(2,1)S(1)}, bf16[4,48,1920]{2,1,0:T(8,128)(2,1)S(1)}, u32[]{:S(2)}, u32[]{:S(2)}) collective-permute-start(bf16[4,48,1920]{2,1,0:T(8,128)(2,1)S(1)} %get-tuple-element.220), channel_id=1, source_target_pairs={{0,4},{1,5},{2,6},{3,7},{4,0},{5,1},{6,2},{7,3},{8,12},{9,13},{10,... | collective-permute-start | bytes 2211848 | tf_op jit(solution)/shard_map/ppermute | solution.py:54
  172.9 36.1 %collective-permute-start.41 = (bf16[4,48,1920]{2,1,0:T(8,128)(2,1)S(1)}, bf16[4,48,1920]{2,1,0:T(8,128)(2,1)S(1)}, u32[]{:S(2)}, u32[]{:S(2)}) collective-permute-start(bf16[4,48,1920]{2,1,0:T(8,128)(2,1)S(1)} %get-tuple-element.219), channel_id=1, source_target_pairs={{0,6},{1,7},{2,4},{3,5},{4,2},{5,3},{6,0},{7,1},{8,14},{9,15},{10,... | collective-permute-start | bytes 2211848 | tf_op jit(solution)/shard_map/ppermute | solution.py:54
  210.2 3.9 %collective-permute-start.45 = (bf16[4,4,48,1152]{3,2,1,0:T(8,128)(2,1)}, bf16[4,4,48,1152]{3,2,1,0:T(8,128)(2,1)S(1)}, u32[]{:S(2)}, u32[]{:S(2)}) collective-permute-start(bf16[4,4,48,1152]{3,2,1,0:T(8,128)(2,1)} %get-tuple-element.186), channel_id=1, source_target_pairs={{0,1},{1,0},{2,3},{3,2},{4,5},{5,4},{6,7},{7,6},{8,9},{9,8},{10,11... | collective-permute-start | bytes 5308424 | tf_op jit(solution)/shard_map/ppermute | solution.py:54
  212.2 7.2 %collective-permute-start.46 = (bf16[48,1920]{1,0:T(8,128)(2,1)S(1)}, bf16[48,1920]{1,0:T(8,128)(2,1)S(1)}, u32[]{:S(2)}, u32[]{:S(2)}) collective-permute-start(bf16[48,1920]{1,0:T(8,128)(2,1)S(1)} %get-tuple-element.232), channel_id=1, source_target_pairs={{0,8},{1,9},{2,10},{3,11},{4,12},{5,13},{6,14},{7,15},{8,0},{9,1},... | collective-permute-start | bytes 552968 | tf_op jit(solution)/shard_map/ppermute | solution.py:54
  214.6 19.1 %collective-permute-start.49 = (bf16[4,48,1152]{2,1,0:T(8,128)(2,1)S(1)}, bf16[4,48,1152]{2,1,0:T(8,128)(2,1)S(1)}, u32[]{:S(2)}, u32[]{:S(2)}) collective-permute-start(bf16[4,48,1152]{2,1,0:T(8,128)(2,1)S(1)} %get-tuple-element.229), channel_id=1, source_target_pairs={{0,2},{1,3},{2,0},{3,1},{4,6},{5,7},{6,4},{7,5},{8,10},{9,11},{10,... | collective-permute-start | bytes 1327112 | tf_op jit(solution)/shard_map/ppermute | solution.py:54
  215.2 21.4 %collective-permute-start.50 = (bf16[4,48,1152]{2,1,0:T(8,128)(2,1)S(1)}, bf16[4,48,1152]{2,1,0:T(8,128)(2,1)S(1)}, u32[]{:S(2)}, u32[]{:S(2)}) collective-permute-start(bf16[4,48,1152]{2,1,0:T(8,128)(2,1)S(1)} %get-tuple-element.228), channel_id=1, source_target_pairs={{0,4},{1,5},{2,6},{3,7},{4,0},{5,1},{6,2},{7,3},{8,12},{9,13},{10,... | collective-permute-start | bytes 1327112 | tf_op jit(solution)/shard_map/ppermute | solution.py:54
  216.4 20.2 %collective-permute-start.51 = (bf16[4,48,1152]{2,1,0:T(8,128)(2,1)S(1)}, bf16[4,48,1152]{2,1,0:T(8,128)(2,1)S(1)}, u32[]{:S(2)}, u32[]{:S(2)}) collective-permute-start(bf16[4,48,1152]{2,1,0:T(8,128)(2,1)S(1)} %get-tuple-element.227), channel_id=1, source_target_pairs={{0,6},{1,7},{2,4},{3,5},{4,2},{5,3},{6,0},{7,1},{8,14},{9,15},{10,... | collective-permute-start | bytes 1327112 | tf_op jit(solution)/shard_map/ppermute | solution.py:54
  218.2 15.6 %collective-permute-start.47 = (bf16[48,1920]{1,0:T(8,128)(2,1)S(1)}, bf16[48,1920]{1,0:T(8,128)(2,1)S(1)}, u32[]{:S(2)}, u32[]{:S(2)}) collective-permute-start(bf16[48,1920]{1,0:T(8,128)(2,1)S(1)} %get-tuple-element.231), channel_id=1, source_target_pairs={{0,16},{1,17},{2,18},{3,19},{4,20},{5,21},{6,22},{7,23},{8,24},{9,... | collective-permute-start | bytes 552968 | tf_op jit(solution)/shard_map/ppermute | solution.py:54
  219.4 14.3 %collective-permute-start.48 = (bf16[48,1920]{1,0:T(8,128)(2,1)S(1)}, bf16[48,1920]{1,0:T(8,128)(2,1)S(1)}, u32[]{:S(2)}, u32[]{:S(2)}) collective-permute-start(bf16[48,1920]{1,0:T(8,128)(2,1)S(1)} %get-tuple-element.230), channel_id=1, source_target_pairs={{0,24},{1,25},{2,26},{3,27},{4,28},{5,29},{6,30},{7,31},{8,16},{9,... | collective-permute-start | bytes 552968 | tf_op jit(solution)/shard_map/ppermute | solution.py:54
  233.7 5.5 %collective-permute-start.62 = (f32[96,384]{1,0:T(8,128)S(1)}, f32[96,384]{1,0:T(8,128)S(1)}, u32[]{:S(2)}, u32[]{:S(2)}) collective-permute-start(f32[96,384]{1,0:T(8,128)S(1)} %slice_select_fusion.2), channel_id=1, source_target_pairs={{0,1},{1,0},{2,3},{3,2},{4,5},{5,4},{6,7},{7,6},{8,9},{9,8},{10,11... | collective-permute-start | bytes 442376 | tf_op jit(solution)/shard_map/ppermute | solution.py:54
  237.9 4.8 %collective-permute-start.52 = (f32[16,288]{1,0:T(8,128)S(1)}, f32[16,288]{1,0:T(8,128)S(1)}, u32[]{:S(2)}, u32[]{:S(2)}) collective-permute-start(f32[16,288]{1,0:T(8,128)S(1)} %slice_select_fusion.6), channel_id=1, source_target_pairs={{0,16},{1,17},{2,18},{3,19},{4,20},{5,21},{6,22},{7,23},{8,24},{9,... | collective-permute-start | bytes 55304 | tf_op jit(solution)/shard_map/ppermute | solution.py:54
  242.7 6.4 %collective-permute-start.53 = (f32[8,288]{1,0:T(8,128)S(1)}, f32[8,288]{1,0:T(8,128)S(1)}, u32[]{:S(2)}, u32[]{:S(2)}) collective-permute-start(f32[8,288]{1,0:T(8,128)S(1)} %slice_select_fusion.7), channel_id=1, source_target_pairs={{0,8},{1,9},{2,10},{3,11},{4,12},{5,13},{6,14},{7,15},{8,0},{9,1},... | collective-permute-start | bytes 27656 | tf_op jit(solution)/shard_map/ppermute | solution.py:54
  244.8 11.8 %collective-permute-start.56 = (bf16[48,1152]{1,0:T(8,128)(2,1)S(1)}, bf16[48,1152]{1,0:T(8,128)(2,1)S(1)}, u32[]{:S(2)}, u32[]{:S(2)}) collective-permute-start(bf16[48,1152]{1,0:T(8,128)(2,1)S(1)} %get-tuple-element.240), channel_id=1, source_target_pairs={{0,8},{1,9},{2,10},{3,11},{4,12},{5,13},{6,14},{7,15},{8,0},{9,1},... | collective-permute-start | bytes 331784 | tf_op jit(solution)/shard_map/ppermute | solution.py:54
  245.5 11.0 %collective-permute-start.57 = (bf16[48,1152]{1,0:T(8,128)(2,1)S(1)}, bf16[48,1152]{1,0:T(8,128)(2,1)S(1)}, u32[]{:S(2)}, u32[]{:S(2)}) collective-permute-start(bf16[48,1152]{1,0:T(8,128)(2,1)S(1)} %get-tuple-element.239), channel_id=1, source_target_pairs={{0,16},{1,17},{2,18},{3,19},{4,20},{5,21},{6,22},{7,23},{8,24},{9,... | collective-permute-start | bytes 331784 | tf_op jit(solution)/shard_map/ppermute | solution.py:54
  246.8 9.8 %collective-permute-start.58 = (bf16[48,1152]{1,0:T(8,128)(2,1)S(1)}, bf16[48,1152]{1,0:T(8,128)(2,1)S(1)}, u32[]{:S(2)}, u32[]{:S(2)}) collective-permute-start(bf16[48,1152]{1,0:T(8,128)(2,1)S(1)} %get-tuple-element.238), channel_id=1, source_target_pairs={{0,24},{1,25},{2,26},{3,27},{4,28},{5,29},{6,30},{7,31},{8,16},{9,... | collective-permute-start | bytes 331784 | tf_op jit(solution)/shard_map/ppermute | solution.py:54
  249.2 3.7 %collective-permute-start.54 = (f32[4,288]{1,0:T(4,128)S(1)}, f32[4,288]{1,0:T(4,128)S(1)}, u32[]{:S(2)}, u32[]{:S(2)}) collective-permute-start(f32[4,288]{1,0:T(4,128)S(1)} %slice_select_fusion.8), channel_id=1, source_target_pairs={{0,4},{1,5},{2,6},{3,7},{4,0},{5,1},{6,2},{7,3},{8,12},{9,13},{10,... | collective-permute-start | bytes 13832 | tf_op jit(solution)/shard_map/ppermute | solution.py:54
  252.9 3.7 %collective-permute-start.55 = (f32[2,288]{1,0:T(2,128)S(1)}, f32[2,288]{1,0:T(2,128)S(1)}, u32[]{:S(2)}, u32[]{:S(2)}) collective-permute-start(f32[2,288]{1,0:T(2,128)S(1)} %broadcast_select_fusion.22), channel_id=1, source_target_pairs={{0,2},{1,3},{2,0},{3,1},{4,6},{5,7},{6,4},{7,5},{8,10},{9,11},{10,... | collective-permute-start | bytes 6920 | tf_op jit(solution)/shard_map/ppermute | solution.py:54
  254.5 5.1 %collective-permute-start.61 = (f32[24,1920]{1,0:T(8,128)S(1)}, f32[24,1920]{1,0:T(8,128)S(1)}, u32[]{:S(2)}, u32[]{:S(2)}) collective-permute-start(f32[24,1920]{1,0:T(8,128)S(1)} %slice_select_fusion), channel_id=1, source_target_pairs={{0,1},{1,0},{2,3},{3,2},{4,5},{5,4},{6,7},{7,6},{8,9},{9,8},{10,11... | collective-permute-start | bytes 552968 | tf_op jit(solution)/shard_map/ppermute | solution.py:54
  256.6 1.2 collective-permute-start.59
  256.8 4.3 %collective-permute-start.60 = (f32[24,1152]{1,0:T(8,128)S(1)}, f32[24,1152]{1,0:T(8,128)S(1)}, u32[]{:S(2)}, u32[]{:S(2)}) collective-permute-start(f32[24,1152]{1,0:T(8,128)S(1)} %slice_select_fusion.4), channel_id=1, source_target_pairs={{0,1},{1,0},{2,3},{3,2},{4,5},{5,4},{6,7},{7,6},{8,9},{9,8},{10,11... | collective-permute-start | bytes 331784 | tf_op jit(solution)/shard_map/ppermute | solution.py:54
  (25 other events, 372.0 us)
where the time goes:
time: 265 us; the launch traced here: 262 us
  Pallas kernels  133 us (50%)
  starting transfers between devices  61.7 us (23%)
  waiting for transfers between devices  44.4 us (17%)
  other arithmetic  14.7 us (6%)
  local copies, waits for them, and re-layouts  6.24 us (2%)
    pallas_call x5, Pallas kernels, kernel_call(): return pl.pallas_call(kernel, **how)(*tie(inputs[:1], *after), *inputs[1:])  132 us
    ppermute x63, starting transfers between devices, swap(): return lax.ppermute(array, AXES, [(i, i ^ bit) for i in range(count)])  61.7 us
    ppermute x63, waiting for transfers between devices, swap(): return lax.ppermute(array, AXES, [(i, i ^ bit) for i in range(count)])  44.4 us
  transfers between devices with their start and end apart: 63, of which 17 were waited for; matrix products, arithmetic and copies ran while one was open for 6% of the time, Pallas kernels for 51%

commit v1 on v0

--- a/solution.py
+++ b/solution.py
@@ -863,11 +863,11 @@
         proj_block = pair_block(proj_weight, core)
         first_column = jnp.stack([first_block] + by_z([first_block] * 3))
         (wide_block,) = tie([wide_block], first_column)
-        first_got, wide_got, (proj_near,) = meet(
-            by_xy([first_column] * 3), by_z([wide_block] * 3), [swap(tie([proj_block], first_column)[0], Z0)]
-        )
+        (proj_block,) = tie([proj_block], first_column)
+        first_got, wide_got = meet(by_xy([first_column] * 3), by_z([wide_block] * 3))
+        proj_near = swap(proj_block, Z0)
         first_pieces = gather_core([first_column, *first_got])
-        wide_column = jnp.stack([wide_block] + wide_got)
+        wide_column, proj_near = tie([jnp.stack([wide_block] + wide_got), proj_near], proj_near)
         wide_got = by_xy([wide_column] * 3)
         (proj_block,) = tie([proj_block], wide_column)
         proj_got = [swap(proj_block, bits) for bits in (Z1, Z0 | Z1)]

time: 265 us -> 265 us (level)
  waiting for transfers between devices: 44.4 us -> 51.4 us
  starting transfers between devices: 61.7 us -> 55.9 us
    ppermute x63, waiting for transfers between devices: 44.4 us -> 51.4 us  [swap(): return lax.ppermute(array, AXES, [(i, i ^ bit) for i in range(count)])]
    ppermute x63, starting transfers between devices: 61.7 us -> 55.9 us  [swap(): return lax.ppermute(array, AXES, [(i, i ^ bit) for i in range(count)])]
  transfers between devices with their start and end apart: 63 -> 63, of which waited for: 17 -> 19; matrix products, arithmetic and copies ran while one was open for 6% -> 6% of each run, Pallas kernels for 51% -> 51%
where the time goes in v1:
time: 265 us; the launch traced here: 262 us
  Pallas kernels  133 us (50%)
  starting transfers between devices  55.9 us (21%)
  waiting for transfers between devices  51.4 us (19%)
  other arithmetic  13.5 us (5%)
  local copies, waits for them, and re-layouts  6.13 us (2%)
    pallas_call x5, Pallas kernels, kernel_call(): return pl.pallas_call(kernel, **how)(*tie(inputs[:1], *after), *inputs[1:])  132 us
    ppermute x63, starting transfers between devices, swap(): return lax.ppermute(array, AXES, [(i, i ^ bit) for i in range(count)])  55.9 us
    ppermute x63, waiting for transfers between devices, swap(): return lax.ppermute(array, AXES, [(i, i ^ bit) for i in range(count)])  51.4 us
  transfers between devices with their start and end apart: 63, of which 19 were waited for; matrix products, arithmetic and copies ran while one was open for 6% of the time, Pallas kernels for 51%

profile of v1, /device:TPU:0, one launch (start us, length us, event | category | flops | bytes accessed | tf_op | source)
XLA Modules:
  0.0 261.8 jit_solution(5952111882059953954)
XLA Ops:
  0.7 0.9 concatenate.37
  1.6 0.9 broadcast_select_fusion.17
  3.0 0.9 collective-permute-done
  3.9 3.0 %collective-permute-start.2 = (bf16[48,1280]{1,0:T(8,128)(2,1)S(1)}, bf16[48,1280]{1,0:T(8,128)(2,1)S(1)}, u32[]{:S(2)}, u32[]{:S(2)}) collective-permute-start(bf16[48,1280]{1,0:T(8,128)(2,1)S(1)} %get-tuple-element.255), channel_id=1, source_target_pairs={{0,8},{1,9},{2,10},{3,11},{4,12},{5,13},{6,14},{7,15},{8,0},{9,1},... | collective-permute-start | bytes 368648 | tf_op jit(solution)/shard_map/ppermute | solution.py:54
  6.9 2.6 collective-permute-start.3
  9.5 0.7 broadcast_select_fusion.20
  10.2 0.9 broadcast_select_fusion.4
  11.8 0.7 broadcast_select_fusion.19
  12.7 0.9 broadcast_select_fusion.3
  13.6 5.6 %collective-permute-done.3 = bf16[48,1280]{1,0:T(8,128)(2,1)S(1)} collective-permute-done((bf16[48,1280]{1,0:T(8,128)(2,1)S(1)}, bf16[48,1280]{1,0:T(8,128)(2,1)S(1)}, u32[]{:S(2)}, u32[]{:S(2)}) %collective-permute-start.3) | collective-permute-done | bytes 122912 | tf_op jit(solution)/shard_map/ppermute | solution.py:54
  19.4 2.2 collective-permute-start.10
  21.6 1.5 collective-permute-start.7
  23.1 1.5 collective-permute-start.8
  25.3 1.2 collective-permute-start.11
  26.5 1.7 collective-permute-start.12
  28.2 11.5 %collective-permute-done.11 = bf16[48,1920]{1,0:T(8,128)(2,1)S(1)} collective-permute-done((bf16[48,1920]{1,0:T(8,128)(2,1)S(1)}, bf16[48,1920]{1,0:T(8,128)(2,1)S(1)}, u32[]{:S(2)}, u32[]{:S(2)}) %collective-permute-start.11) | collective-permute-done | bytes 184352 | tf_op jit(solution)/shard_map/ppermute | solution.py:54
  40.2 5.1 %collective-permute-done.8.rest_2_.rest_5_ = bf16[4,48,1280]{2,1,0:T(8,128)(2,1)} collective-permute-done((bf16[4,48,1280]{2,1,0:T(8,128)(2,1)S(1)}, bf16[4,48,1280]{2,1,0:T(8,128)(2,1)}, u32[]{:S(2)}, u32[]{:S(2)}) %collective-permute-start.8) | collective-permute-done | bytes 491552 | tf_op jit(solution)/shard_map/ppermute | solution.py:54
  46.3 1.0 pad_maximum_fusion.rest_0_
  47.4 4.9 %collective-permute-done.13 = bf16[192,384]{1,0:T(8,128)(2,1)S(1)} collective-permute-done((bf16[192,384]{1,0:T(8,128)(2,1)S(1)}, bf16[192,384]{1,0:T(8,128)(2,1)S(1)}, u32[]{:S(2)}, u32[]{:S(2)}) %collective-permute-start.13) | collective-permute-done | bytes 147488 | tf_op jit(solution)/shard_map/ppermute | solution.py:54
  52.2 1.4 collective-permute-start.21
  53.6 1.3 collective-permute-start.22
  55.0 1.2 collective-permute-start.18
  56.2 0.8 collective-permute-start.19
  57.0 1.4 collective-permute-start.20
  58.5 28.4 %project_attend.1 = (bf16[1024,2304]{1,0:T(8,128)(2,1)}, bf16[1024,768]{1,0:T(8,128)(2,1)}, bf16[1024,768]{1,0:T(8,128)(2,1)S(1)}, f32[6,2,1024]{2,1,0:T(2,128)S(1)}, f32[12,768]{1,0:T(8,128)S(1)}) custom-call(s32[2]{0:T(128)S(1)} %pad_add_fusion.place, bf16[1024,768]{1,0:T(8,128)(2,1)S(1)} %copy-done.5, s32[1024,1]{1,0:T(8,128)S(1)} %copy.29.q_docs.k_docs, ...), custom_call_target="tpu_custom_call" | custom-call | flops 28000000000 | bytes 20000000 | tf_op jit(solution)/shard_map/project_attend/pallas_call | solution.py:111
  87.8 1.6 collective-permute-done.20.rest_3_
  90.0 0.9 collective-permute-start.27
  91.5 1.5 collective-permute-start.28
  93.0 1.2 collective-permute-start.29
  94.2 24.3 %widen.1 = (f32[1024,768]{1,0:T(8,128)}, bf16[1024,768]{1,0:T(8,128)(2,1)S(1)}, bf16[1024,3072]{1,0:T(8,128)(2,1)}, bf16[1024,3072]{1,0:T(8,128)(2,1)}, bf16[4,4...) custom-call(s32[2]{0:T(128)S(1)} %pad_add_fusion.place, bf16[1024,768]{1,0:T(8,128)(2,1)S(1)} %copy-done.5, ...), custom_call_target="tpu_custom_call" | custom-call | flops 10871635968 | bytes 30000000 | tf_op jit(solution)/shard_map/widen/pallas_call | solution.py:111
  118.5 1.0 collective-permute-done.28.rest_10_
  120.6 3.5 %collective-permute-done.30 = bf16[4,4,192,384]{3,2,1,0:T(8,128)(2,1)S(1)} collective-permute-done((bf16[4,4,192,384]{3,2,1,0:T(8,128)(2,1)S(1)}, bf16[4,4,192,384]{3,2,1,0:T(8,128)(2,1)S(1)}, u32[]{:S(2)}, u32[]{:S(2)}) %collective-permute-start.30) | collective-permute-done | bytes 2359328 | tf_op jit(solution)/shard_map/ppermute | solution.py:54
  124.8 1.3 collective-permute-start.35
  126.1 0.8 collective-permute-start.36
  126.9 1.4 collective-permute-start.37
  128.4 33.8 %narrow.1 = (bf16[1024,768]{1,0:T(8,128)(2,1)}, f32[1024,768]{1,0:T(8,128)}, bf16[1024,768]{1,0:T(8,128)(2,1)S(1)}, f32[1,3072]{1,0:T(1,128)S(1)}, f32[1,768]{1,...) custom-call(s32[2]{0:T(128)S(1)} %pad_add_fusion.place, ...), custom_call_target="tpu_custom_call" | custom-call | flops 21743271936 | bytes 40000000 | tf_op jit(solution)/shard_map/narrow/pallas_call | solution.py:111
  163.4 2.3 collective-permute-start.43
  165.6 1.5 collective-permute-start.44
  167.1 0.8 collective-permute-done.38
  168.6 1.3 collective-permute-start.39
  169.9 0.8 collective-permute-start.40
  170.8 1.0 collective-permute-done.42
  171.8 1.5 collective-permute-start.41
  173.3 34.3 %attend_back.1 = (bf16[1024,768]{1,0:T(8,128)(2,1)}, bf16[1024,768]{1,0:T(8,128)(2,1)}, bf16[1024,768]{1,0:T(8,128)(2,1)}, bf16[4,4,48,1152]{3,2,1,0:T(8,128)(2,1)}, bf16[4,4,48,1152]{3,2,1,0:T(8,128)(2,1)}) custom-call(s32[2]{0:T(128)} %copy-done.11, s32[1,1024]{1,0:T(1,128)} %bitcast.150, s32[1024,1]{1,0:T(8,128)} %copy-done, ...), custom_call_target="tpu_custom_call" | custom-call | flops 41999998976 | bytes 20000000 | tf_op jit(solution)/shard_map/attend_back/pallas_call | solution.py:111
  207.7 0.9 copy-done.18
  208.9 2.0 fusion.48
  210.9 1.0 convert_add_fusion.9
  211.9 0.8 collective-permute-done.45
  213.2 1.5 collective-permute-start.49
  215.3 1.5 collective-permute-start.51
  216.8 1.3 collective-permute-start.47
  218.1 2.3 collective-permute-start.48
  220.4 11.3 %first_back.1 = (f32[1024,768]{1,0:T(8,128)}, f32[4,768]{1,0:T(4,128)}) custom-call(s32[2]{0:T(128)} %copy-done.11, bf16[1024,768]{1,0:T(8,128)(2,1)} %x.9, f32[1024,768]{1,0:T(8,128)} %get-tuple-element.193.grad_r, f32[1,768]{1,0:T(1,128)} %get-tuple-element.262.gain, bf16[1024,768]{1,0:T(8,128)(2,1)} %get-tuple-element.194.rest_0_, ...), custom_call_target="tpu_custom_call" | custom-call | flops 3623878656 | bytes 16000000 | tf_op jit(solution)/shard_map/first_back/pallas_call | solution.py:111
  232.4 3.8 %collective-permute-done.50 = bf16[4,48,1152]{2,1,0:T(8,128)(2,1)S(1)} collective-permute-done((bf16[4,48,1152]{2,1,0:T(8,128)(2,1)S(1)}, bf16[4,48,1152]{2,1,0:T(8,128)(2,1)S(1)}, u32[]{:S(2)}, u32[]{:S(2)}) %collective-permute-start.50) | collective-permute-done | bytes 442400 | tf_op jit(solution)/shard_map/ppermute | solution.py:54
  236.4 1.0 pack.1
  237.5 1.4 collective-permute-start.52
  238.9 3.3 %collective-permute-done.52 = f32[16,288]{1,0:T(8,128)S(1)} collective-permute-done((f32[16,288]{1,0:T(8,128)S(1)}, f32[16,288]{1,0:T(8,128)S(1)}, u32[]{:S(2)}, u32[]{:S(2)}) %collective-permute-start.52) | collective-permute-done | bytes 18464 | tf_op jit(solution)/shard_map/ppermute | solution.py:54
  242.3 1.3 collective-permute-start.53
  244.3 0.8 collective-permute-start.56
  245.1 1.4 collective-permute-start.57
  246.4 2.3 collective-permute-start.58
  249.4 3.0 %collective-permute-done.54 = f32[4,288]{1,0:T(4,128)S(1)} collective-permute-done((f32[4,288]{1,0:T(4,128)S(1)}, f32[4,288]{1,0:T(4,128)S(1)}, u32[]{:S(2)}, u32[]{:S(2)}) %collective-permute-start.54) | collective-permute-done | bytes 4640 | tf_op jit(solution)/shard_map/ppermute | solution.py:54
  253.1 3.0 %collective-permute-done.55 = f32[2,288]{1,0:T(2,128)S(1)} collective-permute-done((f32[2,288]{1,0:T(2,128)S(1)}, f32[2,288]{1,0:T(2,128)S(1)}, u32[]{:S(2)}, u32[]{:S(2)}) %collective-permute-start.55) | collective-permute-done | bytes 2336 | tf_op jit(solution)/shard_map/ppermute | solution.py:54
  259.3 0.7 pad_maximum_fusion.3
  (196 shorter events, 18.2 us)
Async XLA Ops:
  2.4 1.4 collective-permute-start
  3.9 9.7 %collective-permute-start.2 = (bf16[48,1280]{1,0:T(8,128)(2,1)S(1)}, bf16[48,1280]{1,0:T(8,128)(2,1)S(1)}, u32[]{:S(2)}, u32[]{:S(2)}) collective-permute-start(bf16[48,1280]{1,0:T(8,128)(2,1)S(1)} %get-tuple-element.255), channel_id=1, source_target_pairs={{0,8},{1,9},{2,10},{3,11},{4,12},{5,13},{6,14},{7,15},{8,0},{9,1},... | collective-permute-start | bytes 368648 | tf_op jit(solution)/shard_map/ppermute | solution.py:54
  6.9 12.4 %collective-permute-start.3 = (bf16[48,1280]{1,0:T(8,128)(2,1)S(1)}, bf16[48,1280]{1,0:T(8,128)(2,1)S(1)}, u32[]{:S(2)}, u32[]{:S(2)}) collective-permute-start(bf16[48,1280]{1,0:T(8,128)(2,1)S(1)} %get-tuple-element.255), channel_id=1, source_target_pairs={{0,16},{1,17},{2,18},{3,19},{4,20},{5,21},{6,22},{7,23},{8,24},{9,... | collective-permute-start | bytes 368648 | tf_op jit(solution)/shard_map/ppermute | solution.py:54
  9.5 9.8 %collective-permute-start.4 = (bf16[48,1280]{1,0:T(8,128)(2,1)S(1)}, bf16[48,1280]{1,0:T(8,128)(2,1)S(1)}, u32[]{:S(2)}, u32[]{:S(2)}) collective-permute-start(bf16[48,1280]{1,0:T(8,128)(2,1)S(1)} %get-tuple-element.255), channel_id=1, source_target_pairs={{0,24},{1,25},{2,26},{3,27},{4,28},{5,29},{6,30},{7,31},{8,16},{9,... | collective-permute-start | bytes 368648 | tf_op jit(solution)/shard_map/ppermute | solution.py:54
  10.2 1.5 collective-permute-start.5
  11.2 1.5 collective-permute-start.6
  19.4 7.1 %collective-permute-start.10 = (bf16[48,1920]{1,0:T(8,128)(2,1)S(1)}, bf16[48,1920]{1,0:T(8,128)(2,1)}, u32[]{:S(2)}, u32[]{:S(2)}) collective-permute-start(bf16[48,1920]{1,0:T(8,128)(2,1)S(1)} %maximum_maximum_fusion), channel_id=1, source_target_pairs={{0,8},{1,9},{2,10},{3,11},{4,12},{5,13},{6,14},{7,15},{8,0},{9,1},... | collective-permute-start | bytes 552968 | tf_op jit(solution)/shard_map/ppermute | solution.py:54
  21.6 18.7 %collective-permute-start.7 = (bf16[4,48,1280]{2,1,0:T(8,128)(2,1)S(1)}, bf16[4,48,1280]{2,1,0:T(8,128)(2,1)S(1)}, u32[]{:S(2)}, u32[]{:S(2)}) collective-permute-start(bf16[4,48,1280]{2,1,0:T(8,128)(2,1)S(1)} %pad_maximum_fusion.2.rest_0_.rest_3_), channel_id=1, source_target_pairs={{0,2},{1,3},{2,0},{3,1},{4,6},{5,7},{6,4},{7,5},{8,10},{9,11},{10,... | collective-permute-start | bytes 1474568 | tf_op jit(solution)/shard_map/ppermute | solution.py:54
  23.1 22.3 %collective-permute-start.8 = (bf16[4,48,1280]{2,1,0:T(8,128)(2,1)S(1)}, bf16[4,48,1280]{2,1,0:T(8,128)(2,1)}, u32[]{:S(2)}, u32[]{:S(2)}) collective-permute-start(bf16[4,48,1280]{2,1,0:T(8,128)(2,1)S(1)} %pad_maximum_fusion.2.rest_0_.rest_3_), channel_id=1, source_target_pairs={{0,4},{1,5},{2,6},{3,7},{4,0},{5,1},{6,2},{7,3},{8,12},{9,13},{10,... | collective-permute-start | bytes 1474568 | tf_op jit(solution)/shard_map/ppermute | solution.py:54
  24.6 20.7 %collective-permute-start.9 = (bf16[4,48,1280]{2,1,0:T(8,128)(2,1)S(1)}, bf16[4,48,1280]{2,1,0:T(8,128)(2,1)}, u32[]{:S(2)}, u32[]{:S(2)}) collective-permute-start(bf16[4,48,1280]{2,1,0:T(8,128)(2,1)S(1)} %pad_maximum_fusion.2.rest_0_.rest_3_), channel_id=1, source_target_pairs={{0,6},{1,7},{2,4},{3,5},{4,2},{5,3},{6,0},{7,1},{8,14},{9,15},{10,... | collective-permute-start | bytes 1474568 | tf_op jit(solution)/shard_map/ppermute | solution.py:54
  25.3 14.3 %collective-permute-start.11 = (bf16[48,1920]{1,0:T(8,128)(2,1)S(1)}, bf16[48,1920]{1,0:T(8,128)(2,1)S(1)}, u32[]{:S(2)}, u32[]{:S(2)}) collective-permute-start(bf16[48,1920]{1,0:T(8,128)(2,1)S(1)} %maximum_maximum_fusion), channel_id=1, source_target_pairs={{0,16},{1,17},{2,18},{3,19},{4,20},{5,21},{6,22},{7,23},{8,24},{9,... | collective-permute-start | bytes 552968 | tf_op jit(solution)/shard_map/ppermute | solution.py:54
  26.5 13.3 %collective-permute-start.12 = (bf16[48,1920]{1,0:T(8,128)(2,1)S(1)}, bf16[48,1920]{1,0:T(8,128)(2,1)S(1)}, u32[]{:S(2)}, u32[]{:S(2)}) collective-permute-start(bf16[48,1920]{1,0:T(8,128)(2,1)S(1)} %maximum_maximum_fusion), channel_id=1, source_target_pairs={{0,24},{1,25},{2,26},{3,27},{4,28},{5,29},{6,30},{7,31},{8,16},{9,... | collective-permute-start | bytes 552968 | tf_op jit(solution)/shard_map/ppermute | solution.py:54
  39.6 6.2 %collective-permute-start.1 = (bf16[96,384]{1,0:T(8,128)(2,1)S(1)}, bf16[96,384]{1,0:T(8,128)(2,1)S(1)}, u32[]{:S(2)}, u32[]{:S(2)}) collective-permute-start(bf16[96,384]{1,0:T(8,128)(2,1)S(1)} %broadcast_select_fusion.10), channel_id=1, source_target_pairs={{0,1},{1,0},{2,3},{3,2},{4,5},{5,4},{6,7},{7,6},{8,9},{9,8},{10,11... | collective-permute-start | bytes 221192 | tf_op jit(solution)/shard_map/ppermute | solution.py:54
  39.7 88.7 %copy-start.11 = (s32[2]{0:T(128)}, s32[2]{0:T(128)S(1)}, u32[]{:S(2)}) copy-start(s32[2]{0:T(128)S(1)} %pad_add_fusion.place) | copy-start | bytes 28
  39.7 13.9 %collective-permute-start.14 = (bf16[4,48,1280]{2,1,0:T(8,128)(2,1)S(1)}, bf16[4,48,1280]{2,1,0:T(8,128)(2,1)S(1)}, u32[]{:S(2)}, u32[]{:S(2)}) collective-permute-start(bf16[4,48,1280]{2,1,0:T(8,128)(2,1)S(1)} %pad_maximum_fusion.2.rest_0_.rest_3_), channel_id=1, source_target_pairs={{0,1},{1,0},{2,3},{3,2},{4,5},{5,4},{6,7},{7,6},{8,9},{9,8},{10,11... | collective-permute-start | bytes 1474568 | tf_op jit(solution)/shard_map/ppermute | solution.py:54
  45.3 9.6 %collective-permute-start.15 = (bf16[4,48,1280]{2,1,0:T(8,128)(2,1)S(1)}, bf16[4,48,1280]{2,1,0:T(8,128)(2,1)S(1)}, u32[]{:S(2)}, u32[]{:S(2)}) collective-permute-start(bf16[4,48,1280]{2,1,0:T(8,128)(2,1)S(1)} %collective-permute-done.7.rest_1_.rest_4_), channel_id=1, source_target_pairs={{0,1},{1,0},{2,3},{3,2},{4,5},{5,4},{6,7},{7,6},{8,9},{9,8},{10,11... | collective-permute-start | bytes 1474568 | tf_op jit(solution)/shard_map/ppermute | solution.py:54
  45.3 10.9 %collective-permute-start.16 = (bf16[4,48,1280]{2,1,0:T(8,128)(2,1)}, bf16[4,48,1280]{2,1,0:T(8,128)(2,1)S(1)}, u32[]{:S(2)}, u32[]{:S(2)}) collective-permute-start(bf16[4,48,1280]{2,1,0:T(8,128)(2,1)} %collective-permute-done.8.rest_2_.rest_5_), channel_id=1, source_target_pairs={{0,1},{1,0},{2,3},{3,2},{4,5},{5,4},{6,7},{7,6},{8,9},{9,8},{10,11... | collective-permute-start | bytes 1474568 | tf_op jit(solution)/shard_map/ppermute | solution.py:54
  45.8 11.2 %collective-permute-start.17 = (bf16[4,48,1280]{2,1,0:T(8,128)(2,1)}, bf16[4,48,1280]{2,1,0:T(8,128)(2,1)S(1)}, u32[]{:S(2)}, u32[]{:S(2)}) collective-permute-start(bf16[4,48,1280]{2,1,0:T(8,128)(2,1)} %collective-permute-done.9.rest_3_.rest_6_), channel_id=1, source_target_pairs={{0,1},{1,0},{2,3},{3,2},{4,5},{5,4},{6,7},{7,6},{8,9},{9,8},{10,11... | collective-permute-start | bytes 1474568 | tf_op jit(solution)/shard_map/ppermute | solution.py:54
  45.9 6.3 %collective-permute-start.13 = (bf16[192,384]{1,0:T(8,128)(2,1)S(1)}, bf16[192,384]{1,0:T(8,128)(2,1)S(1)}, u32[]{:S(2)}, u32[]{:S(2)}) collective-permute-start(bf16[192,384]{1,0:T(8,128)(2,1)S(1)} %pad_maximum_fusion.5), channel_id=1, source_target_pairs={{0,8},{1,9},{2,10},{3,11},{4,12},{5,13},{6,14},{7,15},{8,0},{9,1},... | collective-permute-start | bytes 442376 | tf_op jit(solution)/shard_map/ppermute | solution.py:54
  52.2 35.4 %collective-permute-start.21 = (bf16[192,384]{1,0:T(8,128)(2,1)S(1)}, bf16[192,384]{1,0:T(8,128)(2,1)S(1)}, u32[]{:S(2)}, u32[]{:S(2)}) collective-permute-start(bf16[192,384]{1,0:T(8,128)(2,1)S(1)} %pad_maximum_fusion.5), channel_id=1, source_target_pairs={{0,16},{1,17},{2,18},{3,19},{4,20},{5,21},{6,22},{7,23},{8,24},{9,... | collective-permute-start | bytes 442376 | tf_op jit(solution)/shard_map/ppermute | solution.py:54
  53.6 34.0 %collective-permute-start.22 = (bf16[192,384]{1,0:T(8,128)(2,1)S(1)}, bf16[192,384]{1,0:T(8,128)(2,1)S(1)}, u32[]{:S(2)}, u32[]{:S(2)}) collective-permute-start(bf16[192,384]{1,0:T(8,128)(2,1)S(1)} %pad_maximum_fusion.5), channel_id=1, source_target_pairs={{0,24},{1,25},{2,26},{3,27},{4,28},{5,29},{6,30},{7,31},{8,16},{9,... | collective-permute-start | bytes 442376 | tf_op jit(solution)/shard_map/ppermute | solution.py:54
  55.0 32.7 %collective-permute-start.18 = (bf16[4,48,1920]{2,1,0:T(8,128)(2,1)S(1)}, bf16[4,48,1920]{2,1,0:T(8,128)(2,1)S(1)}, u32[]{:S(2)}, u32[]{:S(2)}) collective-permute-start(bf16[4,48,1920]{2,1,0:T(8,128)(2,1)S(1)} %pad_maximum_fusion.rest_0_), channel_id=1, source_target_pairs={{0,2},{1,3},{2,0},{3,1},{4,6},{5,7},{6,4},{7,5},{8,10},{9,11},{10,... | collective-permute-start | bytes 2211848 | tf_op jit(solution)/shard_map/ppermute | solution.py:54
  56.2 31.6 %collective-permute-start.19 = (bf16[4,48,1920]{2,1,0:T(8,128)(2,1)S(1)}, bf16[4,48,1920]{2,1,0:T(8,128)(2,1)S(1)}, u32[]{:S(2)}, u32[]{:S(2)}) collective-permute-start(bf16[4,48,1920]{2,1,0:T(8,128)(2,1)S(1)} %pad_maximum_fusion.rest_0_), channel_id=1, source_target_pairs={{0,4},{1,5},{2,6},{3,7},{4,0},{5,1},{6,2},{7,3},{8,12},{9,13},{10,... | collective-permute-start | bytes 2211848 | tf_op jit(solution)/shard_map/ppermute | solution.py:54
  57.0 32.4 %collective-permute-start.20 = (bf16[4,48,1920]{2,1,0:T(8,128)(2,1)S(1)}, bf16[4,48,1920]{2,1,0:T(8,128)(2,1)S(1)}, u32[]{:S(2)}, u32[]{:S(2)}) collective-permute-start(bf16[4,48,1920]{2,1,0:T(8,128)(2,1)S(1)} %pad_maximum_fusion.rest_0_), channel_id=1, source_target_pairs={{0,6},{1,7},{2,4},{3,5},{4,2},{5,3},{6,0},{7,1},{8,14},{9,15},{10,... | collective-permute-start | bytes 2211848 | tf_op jit(solution)/shard_map/ppermute | solution.py:54
  87.6 3.9 %collective-permute-start.23 = (bf16[4,48,1920]{2,1,0:T(8,128)(2,1)S(1)}, bf16[4,48,1920]{2,1,0:T(8,128)(2,1)S(1)}, u32[]{:S(2)}, u32[]{:S(2)}) collective-permute-start(bf16[4,48,1920]{2,1,0:T(8,128)(2,1)S(1)} %pad_maximum_fusion.rest_0_), channel_id=1, source_target_pairs={{0,1},{1,0},{2,3},{3,2},{4,5},{5,4},{6,7},{7,6},{8,9},{9,8},{10,11... | collective-permute-start | bytes 2211848 | tf_op jit(solution)/shard_map/ppermute | solution.py:54
  89.4 3.6 %collective-permute-start.24 = (bf16[4,48,1920]{2,1,0:T(8,128)(2,1)S(1)}, bf16[4,48,1920]{2,1,0:T(8,128)(2,1)S(1)}, u32[]{:S(2)}, u32[]{:S(2)}) collective-permute-start(bf16[4,48,1920]{2,1,0:T(8,128)(2,1)S(1)} %collective-permute-done.18.rest_1_), channel_id=1, source_target_pairs={{0,1},{1,0},{2,3},{3,2},{4,5},{5,4},{6,7},{7,6},{8,9},{9,8},{10,11... | collective-permute-start | bytes 2211848 | tf_op jit(solution)/shard_map/ppermute | solution.py:54
  89.4 4.8 %collective-permute-start.25 = (bf16[4,48,1920]{2,1,0:T(8,128)(2,1)S(1)}, bf16[4,48,1920]{2,1,0:T(8,128)(2,1)S(1)}, u32[]{:S(2)}, u32[]{:S(2)}) collective-permute-start(bf16[4,48,1920]{2,1,0:T(8,128)(2,1)S(1)} %collective-permute-done.19.rest_2_), channel_id=1, source_target_pairs={{0,1},{1,0},{2,3},{3,2},{4,5},{5,4},{6,7},{7,6},{8,9},{9,8},{10,11... | collective-permute-start | bytes 2211848 | tf_op jit(solution)/shard_map/ppermute | solution.py:54
  89.9 4.3 %collective-permute-start.26 = (bf16[4,48,1920]{2,1,0:T(8,128)(2,1)S(1)}, bf16[4,48,1920]{2,1,0:T(8,128)(2,1)S(1)}, u32[]{:S(2)}, u32[]{:S(2)}) collective-permute-start(bf16[4,48,1920]{2,1,0:T(8,128)(2,1)S(1)} %collective-permute-done.20.rest_3_), channel_id=1, source_target_pairs={{0,1},{1,0},{2,3},{3,2},{4,5},{5,4},{6,7},{7,6},{8,9},{9,8},{10,11... | collective-permute-start | bytes 2211848 | tf_op jit(solution)/shard_map/ppermute | solution.py:54
  90.0 28.5 %collective-permute-start.27 = (bf16[4,192,384]{2,1,0:T(8,128)(2,1)S(1)}, bf16[4,192,384]{2,1,0:T(8,128)(2,1)S(1)}, u32[]{:S(2)}, u32[]{:S(2)}) collective-permute-start(bf16[4,192,384]{2,1,0:T(8,128)(2,1)S(1)} %pad_maximum_fusion.1.rest_8_), channel_id=1, source_target_pairs={{0,2},{1,3},{2,0},{3,1},{4,6},{5,7},{6,4},{7,5},{8,10},{9,11},{10,... | collective-permute-start | bytes 1769480 | tf_op jit(solution)/shard_map/ppermute | solution.py:54
  91.5 28.1 %collective-permute-start.28 = (bf16[4,192,384]{2,1,0:T(8,128)(2,1)S(1)}, bf16[4,192,384]{2,1,0:T(8,128)(2,1)S(1)}, u32[]{:S(2)}, u32[]{:S(2)}) collective-permute-start(bf16[4,192,384]{2,1,0:T(8,128)(2,1)S(1)} %pad_maximum_fusion.1.rest_8_), channel_id=1, source_target_pairs={{0,4},{1,5},{2,6},{3,7},{4,0},{5,1},{6,2},{7,3},{8,12},{9,13},{10,... | collective-permute-start | bytes 1769480 | tf_op jit(solution)/shard_map/ppermute | solution.py:54
  93.0 26.6 %collective-permute-start.29 = (bf16[4,192,384]{2,1,0:T(8,128)(2,1)S(1)}, bf16[4,192,384]{2,1,0:T(8,128)(2,1)S(1)}, u32[]{:S(2)}, u32[]{:S(2)}) collective-permute-start(bf16[4,192,384]{2,1,0:T(8,128)(2,1)S(1)} %pad_maximum_fusion.1.rest_8_), channel_id=1, source_target_pairs={{0,6},{1,7},{2,4},{3,5},{4,2},{5,3},{6,0},{7,1},{8,14},{9,15},{10,... | collective-permute-start | bytes 1769480 | tf_op jit(solution)/shard_map/ppermute | solution.py:54
  119.6 4.5 %collective-permute-start.30 = (bf16[4,4,192,384]{3,2,1,0:T(8,128)(2,1)S(1)}, bf16[4,4,192,384]{3,2,1,0:T(8,128)(2,1)S(1)}, u32[]{:S(2)}, u32[]{:S(2)}) collective-permute-start(bf16[4,4,192,384]{3,2,1,0:T(8,128)(2,1)S(1)} %get-tuple-element.152), channel_id=1, source_target_pairs={{0,1},{1,0},{2,3},{3,2},{4,5},{5,4},{6,7},{7,6},{8,9},{9,8},{10,11... | collective-permute-start | bytes 7077896 | tf_op jit(solution)/shard_map/ppermute | solution.py:54
  119.6 6.5 %collective-permute-start.31 = (bf16[4,192,384]{2,1,0:T(8,128)(2,1)S(1)}, bf16[4,192,384]{2,1,0:T(8,128)(2,1)S(1)}, u32[]{:S(2)}, u32[]{:S(2)}) collective-permute-start(bf16[4,192,384]{2,1,0:T(8,128)(2,1)S(1)} %pad_maximum_fusion.1.rest_8_), channel_id=1, source_target_pairs={{0,1},{1,0},{2,3},{3,2},{4,5},{5,4},{6,7},{7,6},{8,9},{9,8},{10,11... | collective-permute-start | bytes 1769480 | tf_op jit(solution)/shard_map/ppermute | solution.py:54
  120.1 6.9 %collective-permute-start.32 = (bf16[4,192,384]{2,1,0:T(8,128)(2,1)S(1)}, bf16[4,192,384]{2,1,0:T(8,128)(2,1)S(1)}, u32[]{:S(2)}, u32[]{:S(2)}) collective-permute-start(bf16[4,192,384]{2,1,0:T(8,128)(2,1)S(1)} %collective-permute-done.27.rest_9_), channel_id=1, source_target_pairs={{0,1},{1,0},{2,3},{3,2},{4,5},{5,4},{6,7},{7,6},{8,9},{9,8},{10,11... | collective-permute-start | bytes 1769480 | tf_op jit(solution)/shard_map/ppermute | solution.py:54
  120.1 8.3 %collective-permute-start.33 = (bf16[4,192,384]{2,1,0:T(8,128)(2,1)S(1)}, bf16[4,192,384]{2,1,0:T(8,128)(2,1)S(1)}, u32[]{:S(2)}, u32[]{:S(2)}) collective-permute-start(bf16[4,192,384]{2,1,0:T(8,128)(2,1)S(1)} %collective-permute-done.28.rest_10_), channel_id=1, source_target_pairs={{0,1},{1,0},{2,3},{3,2},{4,5},{5,4},{6,7},{7,6},{8,9},{9,8},{10,11... | collective-permute-start | bytes 1769480 | tf_op jit(solution)/shard_map/ppermute | solution.py:54
  120.6 7.8 %collective-permute-start.34 = (bf16[4,192,384]{2,1,0:T(8,128)(2,1)S(1)}, bf16[4,192,384]{2,1,0:T(8,128)(2,1)S(1)}, u32[]{:S(2)}, u32[]{:S(2)}) collective-permute-start(bf16[4,192,384]{2,1,0:T(8,128)(2,1)S(1)} %collective-permute-done.29.rest_11_), channel_id=1, source_target_pairs={{0,1},{1,0},{2,3},{3,2},{4,5},{5,4},{6,7},{7,6},{8,9},{9,8},{10,11... | collective-permute-start | bytes 1769480 | tf_op jit(solution)/shard_map/ppermute | solution.py:54
  124.8 37.4 %collective-permute-start.35 = (bf16[4,192,384]{2,1,0:T(8,128)(2,1)S(1)}, bf16[4,192,384]{2,1,0:T(8,128)(2,1)S(1)}, u32[]{:S(2)}, u32[]{:S(2)}) collective-permute-start(bf16[4,192,384]{2,1,0:T(8,128)(2,1)S(1)} %get-tuple-element.227), channel_id=1, source_target_pairs={{0,2},{1,3},{2,0},{3,1},{4,6},{5,7},{6,4},{7,5},{8,10},{9,11},{10,... | collective-permute-start | bytes 1769480 | tf_op jit(solution)/shard_map/ppermute | solution.py:54
  126.1 36.1 %collective-permute-start.36 = (bf16[4,192,384]{2,1,0:T(8,128)(2,1)S(1)}, bf16[4,192,384]{2,1,0:T(8,128)(2,1)S(1)}, u32[]{:S(2)}, u32[]{:S(2)}) collective-permute-start(bf16[4,192,384]{2,1,0:T(8,128)(2,1)S(1)} %get-tuple-element.226), channel_id=1, source_target_pairs={{0,4},{1,5},{2,6},{3,7},{4,0},{5,1},{6,2},{7,3},{8,12},{9,13},{10,... | collective-permute-start | bytes 1769480 | tf_op jit(solution)/shard_map/ppermute | solution.py:54
  126.9 35.3 %collective-permute-start.37 = (bf16[4,192,384]{2,1,0:T(8,128)(2,1)S(1)}, bf16[4,192,384]{2,1,0:T(8,128)(2,1)S(1)}, u32[]{:S(2)}, u32[]{:S(2)}) collective-permute-start(bf16[4,192,384]{2,1,0:T(8,128)(2,1)S(1)} %get-tuple-element.225), channel_id=1, source_target_pairs={{0,6},{1,7},{2,4},{3,5},{4,2},{5,3},{6,0},{7,1},{8,14},{9,15},{10,... | collective-permute-start | bytes 1769480 | tf_op jit(solution)/shard_map/ppermute | solution.py:54
  162.2 5.7 %collective-permute-start.38 = (bf16[4,4,48,1920]{3,2,1,0:T(8,128)(2,1)}, bf16[4,4,48,1920]{3,2,1,0:T(8,128)(2,1)S(1)}, u32[]{:S(2)}, u32[]{:S(2)}) collective-permute-start(bf16[4,4,48,1920]{3,2,1,0:T(8,128)(2,1)} %get-tuple-element.176), channel_id=1, source_target_pairs={{0,1},{1,0},{2,3},{3,2},{4,5},{5,4},{6,7},{7,6},{8,9},{9,8},{10,11... | collective-permute-start | bytes 8847368 | tf_op jit(solution)/shard_map/ppermute | solution.py:54
  162.6 9.2 %collective-permute-start.42 = (bf16[192,384]{1,0:T(8,128)(2,1)S(1)}, bf16[192,384]{1,0:T(8,128)(2,1)}, u32[]{:S(2)}, u32[]{:S(2)}) collective-permute-start(bf16[192,384]{1,0:T(8,128)(2,1)S(1)} %get-tuple-element.238), channel_id=1, source_target_pairs={{0,8},{1,9},{2,10},{3,11},{4,12},{5,13},{6,14},{7,15},{8,0},{9,1},... | collective-permute-start | bytes 442376 | tf_op jit(solution)/shard_map/ppermute | solution.py:54
  163.4 44.2 %collective-permute-start.43 = (bf16[192,384]{1,0:T(8,128)(2,1)S(1)}, bf16[192,384]{1,0:T(8,128)(2,1)S(1)}, u32[]{:S(2)}, u32[]{:S(2)}) collective-permute-start(bf16[192,384]{1,0:T(8,128)(2,1)S(1)} %get-tuple-element.237), channel_id=1, source_target_pairs={{0,16},{1,17},{2,18},{3,19},{4,20},{5,21},{6,22},{7,23},{8,24},{9,... | collective-permute-start | bytes 442376 | tf_op jit(solution)/shard_map/ppermute | solution.py:54
  165.6 42.0 %collective-permute-start.44 = (bf16[192,384]{1,0:T(8,128)(2,1)S(1)}, bf16[192,384]{1,0:T(8,128)(2,1)S(1)}, u32[]{:S(2)}, u32[]{:S(2)}) collective-permute-start(bf16[192,384]{1,0:T(8,128)(2,1)S(1)} %get-tuple-element.236), channel_id=1, source_target_pairs={{0,24},{1,25},{2,26},{3,27},{4,28},{5,29},{6,30},{7,31},{8,16},{9,... | collective-permute-start | bytes 442376 | tf_op jit(solution)/shard_map/ppermute | solution.py:54
  168.6 39.0 %collective-permute-start.39 = (bf16[4,48,1920]{2,1,0:T(8,128)(2,1)S(1)}, bf16[4,48,1920]{2,1,0:T(8,128)(2,1)S(1)}, u32[]{:S(2)}, u32[]{:S(2)}) collective-permute-start(bf16[4,48,1920]{2,1,0:T(8,128)(2,1)S(1)} %get-tuple-element.223), channel_id=1, source_target_pairs={{0,2},{1,3},{2,0},{3,1},{4,6},{5,7},{6,4},{7,5},{8,10},{9,11},{10,... | collective-permute-start | bytes 2211848 | tf_op jit(solution)/shard_map/ppermute | solution.py:54
  169.9 37.7 %collective-permute-start.40 = (bf16[4,48,1920]{2,1,0:T(8,128)(2,1)S(1)}, bf16[4,48,1920]{2,1,0:T(8,128)(2,1)S(1)}, u32[]{:S(2)}, u32[]{:S(2)}) collective-permute-start(bf16[4,48,1920]{2,1,0:T(8,128)(2,1)S(1)} %get-tuple-element.222), channel_id=1, source_target_pairs={{0,4},{1,5},{2,6},{3,7},{4,0},{5,1},{6,2},{7,3},{8,12},{9,13},{10,... | collective-permute-start | bytes 2211848 | tf_op jit(solution)/shard_map/ppermute | solution.py:54
  171.8 35.9 %collective-permute-start.41 = (bf16[4,48,1920]{2,1,0:T(8,128)(2,1)S(1)}, bf16[4,48,1920]{2,1,0:T(8,128)(2,1)S(1)}, u32[]{:S(2)}, u32[]{:S(2)}) collective-permute-start(bf16[4,48,1920]{2,1,0:T(8,128)(2,1)S(1)} %get-tuple-element.221), channel_id=1, source_target_pairs={{0,6},{1,7},{2,4},{3,5},{4,2},{5,3},{6,0},{7,1},{8,14},{9,15},{10,... | collective-permute-start | bytes 2211848 | tf_op jit(solution)/shard_map/ppermute | solution.py:54
  208.8 3.9 %collective-permute-start.45 = (bf16[4,4,48,1152]{3,2,1,0:T(8,128)(2,1)}, bf16[4,4,48,1152]{3,2,1,0:T(8,128)(2,1)S(1)}, u32[]{:S(2)}, u32[]{:S(2)}) collective-permute-start(bf16[4,4,48,1152]{3,2,1,0:T(8,128)(2,1)} %get-tuple-element.188), channel_id=1, source_target_pairs={{0,1},{1,0},{2,3},{3,2},{4,5},{5,4},{6,7},{7,6},{8,9},{9,8},{10,11... | collective-permute-start | bytes 5308424 | tf_op jit(solution)/shard_map/ppermute | solution.py:54
  210.8 7.3 %collective-permute-start.46 = (bf16[48,1920]{1,0:T(8,128)(2,1)S(1)}, bf16[48,1920]{1,0:T(8,128)(2,1)S(1)}, u32[]{:S(2)}, u32[]{:S(2)}) collective-permute-start(bf16[48,1920]{1,0:T(8,128)(2,1)S(1)} %get-tuple-element.234), channel_id=1, source_target_pairs={{0,8},{1,9},{2,10},{3,11},{4,12},{5,13},{6,14},{7,15},{8,0},{9,1},... | collective-permute-start | bytes 552968 | tf_op jit(solution)/shard_map/ppermute | solution.py:54
  213.2 19.1 %collective-permute-start.49 = (bf16[4,48,1152]{2,1,0:T(8,128)(2,1)S(1)}, bf16[4,48,1152]{2,1,0:T(8,128)(2,1)S(1)}, u32[]{:S(2)}, u32[]{:S(2)}) collective-permute-start(bf16[4,48,1152]{2,1,0:T(8,128)(2,1)S(1)} %get-tuple-element.231), channel_id=1, source_target_pairs={{0,2},{1,3},{2,0},{3,1},{4,6},{5,7},{6,4},{7,5},{8,10},{9,11},{10,... | collective-permute-start | bytes 1327112 | tf_op jit(solution)/shard_map/ppermute | solution.py:54
  214.8 21.4 %collective-permute-start.50 = (bf16[4,48,1152]{2,1,0:T(8,128)(2,1)S(1)}, bf16[4,48,1152]{2,1,0:T(8,128)(2,1)S(1)}, u32[]{:S(2)}, u32[]{:S(2)}) collective-permute-start(bf16[4,48,1152]{2,1,0:T(8,128)(2,1)S(1)} %get-tuple-element.230), channel_id=1, source_target_pairs={{0,4},{1,5},{2,6},{3,7},{4,0},{5,1},{6,2},{7,3},{8,12},{9,13},{10,... | collective-permute-start | bytes 1327112 | tf_op jit(solution)/shard_map/ppermute | solution.py:54
  215.3 20.9 %collective-permute-start.51 = (bf16[4,48,1152]{2,1,0:T(8,128)(2,1)S(1)}, bf16[4,48,1152]{2,1,0:T(8,128)(2,1)S(1)}, u32[]{:S(2)}, u32[]{:S(2)}) collective-permute-start(bf16[4,48,1152]{2,1,0:T(8,128)(2,1)S(1)} %get-tuple-element.229), channel_id=1, source_target_pairs={{0,6},{1,7},{2,4},{3,5},{4,2},{5,3},{6,0},{7,1},{8,14},{9,15},{10,... | collective-permute-start | bytes 1327112 | tf_op jit(solution)/shard_map/ppermute | solution.py:54
  216.8 15.6 %collective-permute-start.47 = (bf16[48,1920]{1,0:T(8,128)(2,1)S(1)}, bf16[48,1920]{1,0:T(8,128)(2,1)S(1)}, u32[]{:S(2)}, u32[]{:S(2)}) collective-permute-start(bf16[48,1920]{1,0:T(8,128)(2,1)S(1)} %get-tuple-element.233), channel_id=1, source_target_pairs={{0,16},{1,17},{2,18},{3,19},{4,20},{5,21},{6,22},{7,23},{8,24},{9,... | collective-permute-start | bytes 552968 | tf_op jit(solution)/shard_map/ppermute | solution.py:54
  218.1 14.2 %collective-permute-start.48 = (bf16[48,1920]{1,0:T(8,128)(2,1)S(1)}, bf16[48,1920]{1,0:T(8,128)(2,1)S(1)}, u32[]{:S(2)}, u32[]{:S(2)}) collective-permute-start(bf16[48,1920]{1,0:T(8,128)(2,1)S(1)} %get-tuple-element.232), channel_id=1, source_target_pairs={{0,24},{1,25},{2,26},{3,27},{4,28},{5,29},{6,30},{7,31},{8,16},{9,... | collective-permute-start | bytes 552968 | tf_op jit(solution)/shard_map/ppermute | solution.py:54
  232.3 6.5 %collective-permute-start.62 = (f32[96,384]{1,0:T(8,128)S(1)}, f32[96,384]{1,0:T(8,128)S(1)}, u32[]{:S(2)}, u32[]{:S(2)}) collective-permute-start(f32[96,384]{1,0:T(8,128)S(1)} %slice_select_fusion.2), channel_id=1, source_target_pairs={{0,1},{1,0},{2,3},{3,2},{4,5},{5,4},{6,7},{7,6},{8,9},{9,8},{10,11... | collective-permute-start | bytes 442376 | tf_op jit(solution)/shard_map/ppermute | solution.py:54
  237.5 4.8 %collective-permute-start.52 = (f32[16,288]{1,0:T(8,128)S(1)}, f32[16,288]{1,0:T(8,128)S(1)}, u32[]{:S(2)}, u32[]{:S(2)}) collective-permute-start(f32[16,288]{1,0:T(8,128)S(1)} %slice_select_fusion.6), channel_id=1, source_target_pairs={{0,16},{1,17},{2,18},{3,19},{4,20},{5,21},{6,22},{7,23},{8,24},{9,... | collective-permute-start | bytes 55304 | tf_op jit(solution)/shard_map/ppermute | solution.py:54
  242.3 6.4 %collective-permute-start.53 = (f32[8,288]{1,0:T(8,128)S(1)}, f32[8,288]{1,0:T(8,128)S(1)}, u32[]{:S(2)}, u32[]{:S(2)}) collective-permute-start(f32[8,288]{1,0:T(8,128)S(1)} %slice_select_fusion.7), channel_id=1, source_target_pairs={{0,8},{1,9},{2,10},{3,11},{4,12},{5,13},{6,14},{7,15},{8,0},{9,1},... | collective-permute-start | bytes 27656 | tf_op jit(solution)/shard_map/ppermute | solution.py:54
  244.3 11.8 %collective-permute-start.56 = (bf16[48,1152]{1,0:T(8,128)(2,1)S(1)}, bf16[48,1152]{1,0:T(8,128)(2,1)S(1)}, u32[]{:S(2)}, u32[]{:S(2)}) collective-permute-start(bf16[48,1152]{1,0:T(8,128)(2,1)S(1)} %get-tuple-element.242), channel_id=1, source_target_pairs={{0,8},{1,9},{2,10},{3,11},{4,12},{5,13},{6,14},{7,15},{8,0},{9,1},... | collective-permute-start | bytes 331784 | tf_op jit(solution)/shard_map/ppermute | solution.py:54
  245.1 11.0 %collective-permute-start.57 = (bf16[48,1152]{1,0:T(8,128)(2,1)S(1)}, bf16[48,1152]{1,0:T(8,128)(2,1)S(1)}, u32[]{:S(2)}, u32[]{:S(2)}) collective-permute-start(bf16[48,1152]{1,0:T(8,128)(2,1)S(1)} %get-tuple-element.241), channel_id=1, source_target_pairs={{0,16},{1,17},{2,18},{3,19},{4,20},{5,21},{6,22},{7,23},{8,24},{9,... | collective-permute-start | bytes 331784 | tf_op jit(solution)/shard_map/ppermute | solution.py:54
  246.4 9.7 %collective-permute-start.58 = (bf16[48,1152]{1,0:T(8,128)(2,1)S(1)}, bf16[48,1152]{1,0:T(8,128)(2,1)S(1)}, u32[]{:S(2)}, u32[]{:S(2)}) collective-permute-start(bf16[48,1152]{1,0:T(8,128)(2,1)S(1)} %get-tuple-element.240), channel_id=1, source_target_pairs={{0,24},{1,25},{2,26},{3,27},{4,28},{5,29},{6,30},{7,31},{8,16},{9,... | collective-permute-start | bytes 331784 | tf_op jit(solution)/shard_map/ppermute | solution.py:54
  248.7 3.7 %collective-permute-start.54 = (f32[4,288]{1,0:T(4,128)S(1)}, f32[4,288]{1,0:T(4,128)S(1)}, u32[]{:S(2)}, u32[]{:S(2)}) collective-permute-start(f32[4,288]{1,0:T(4,128)S(1)} %slice_select_fusion.8), channel_id=1, source_target_pairs={{0,4},{1,5},{2,6},{3,7},{4,0},{5,1},{6,2},{7,3},{8,12},{9,13},{10,... | collective-permute-start | bytes 13832 | tf_op jit(solution)/shard_map/ppermute | solution.py:54
  252.4 3.7 %collective-permute-start.55 = (f32[2,288]{1,0:T(2,128)S(1)}, f32[2,288]{1,0:T(2,128)S(1)}, u32[]{:S(2)}, u32[]{:S(2)}) collective-permute-start(f32[2,288]{1,0:T(2,128)S(1)} %broadcast_select_fusion.22), channel_id=1, source_target_pairs={{0,2},{1,3},{2,0},{3,1},{4,6},{5,7},{6,4},{7,5},{8,10},{9,11},{10,... | collective-permute-start | bytes 6920 | tf_op jit(solution)/shard_map/ppermute | solution.py:54
  253.1 6.1 %collective-permute-start.61 = (f32[24,1920]{1,0:T(8,128)S(1)}, f32[24,1920]{1,0:T(8,128)S(1)}, u32[]{:S(2)}, u32[]{:S(2)}) collective-permute-start(f32[24,1920]{1,0:T(8,128)S(1)} %slice_select_fusion), channel_id=1, source_target_pairs={{0,1},{1,0},{2,3},{3,2},{4,5},{5,4},{6,7},{7,6},{8,9},{9,8},{10,11... | collective-permute-start | bytes 552968 | tf_op jit(solution)/shard_map/ppermute | solution.py:54
  256.2 1.2 collective-permute-start.59
  256.3 4.3 %collective-permute-start.60 = (f32[24,1152]{1,0:T(8,128)S(1)}, f32[24,1152]{1,0:T(8,128)S(1)}, u32[]{:S(2)}, u32[]{:S(2)}) collective-permute-start(f32[24,1152]{1,0:T(8,128)S(1)} %slice_select_fusion.4), channel_id=1, source_target_pairs={{0,1},{1,0},{2,3},{3,2},{4,5},{5,4},{6,7},{7,6},{8,9},{9,8},{10,11... | collective-permute-start | bytes 331784 | tf_op jit(solution)/shard_map/ppermute | solution.py:54
  (25 other events, 492.8 us)
